TPU v7x, 256 devices: a whole 4x4x8 slice. The times are simulated.
256 devices in a mesh: group: 8 (over y, x_hi), table: 32 (over z, x_lo, core).
Axes of the slice: x: 4 (x_hi: 2, x_lo: 2; x = x_hi * 2 + x_lo), y: 4, z: 8, core: 2. Of those that a mesh axis runs over, the one named last changes fastest.
Arguments:
- table_rows: float32 [8, 131072, 128], P('group', 'table'), may hold values from -6 to 6
- row_state: float32 [8, 131072], P('group', 'table'), may hold values from 0.0001 to 0.01
- parity: float32 [32, 32, 64, 128], P('table', 'group'), may hold values from -24 to 24
- parity_slot: int32 [32, 32], P('table'), may hold values from 0 to 31, each once within a row
- row_shard: int32 [8, 16384, 16, 1], P('group', 'table'), may hold values from 0 to 31; in each aligned block of 8192 rows (0 to 8191, 8192 to 16383, ..., all dimensions but the last counted through in order) at most 512 rows name the same one
- row_offset: int32 [8, 16384, 16], P('group', 'table'), may hold values from 0 to 255
- labels: int32 [16384], P('table'), may hold values 0 or 1
- first_weight: bfloat16 [16384, 1024], P('group'), may hold values from -0.046875 to 0.046875
- last_weight: float32 [1024], replicated, may hold values from -0.1875 to 0.1875
Outputs:
- updated_rows: float32 [8, 131072, 128], P('group', 'table')
- updated_state: float32 [8, 131072], P('group', 'table')
- updated_parity: float32 [32, 32, 64, 128], P('table', 'group')
- first_grad: float32 [1024, 16384], P('table', 'group')
Inputs may be any that keep to these rules, and one draw needn't show every extreme that they name: `row_shard`: among the 8192 lookups of one group index and one aligned block of 512 samples, no table index is named more than 512 times, a bound that some block reaches. `parity_slot`: each row names every slot once.
All inputs are finite; a program needn't handle non-finite values. No bound on the sum of `labels` on one device may be relied on, other than what follows from the above.
Results may differ from a plain program's by a relative error of at most 0.0007.
The roundings to bfloat16 on the way count: a program that leaves them out, or rounds other values in their place, can miss the bound.
Values may be sent and summed in bfloat16 or wider, within the bound.
A program may use at most 64 MiB of HBM per device.

v0:
```python
import jax
import jax.numpy as jnp
from jax import lax
from jax.sharding import PartitionSpec as P

LEARN_RATE = 0.1


def head_slope(pre_act, label_rows, last_weight):
    activated = jax.nn.silu(pre_act)
    logits = jnp.dot(activated, last_weight, precision=lax.Precision.HIGHEST)
    residual = jax.nn.sigmoid(logits) - label_rows.astype(jnp.float32)
    sig_pre = jax.nn.sigmoid(pre_act)
    return (
        residual[:, None] * last_weight[None, :] * (sig_pre * (1.0 + pre_act * (1.0 - sig_pre)))
    ).astype(jnp.bfloat16)


def weight_gradient(back_slope, pooled):
    return lax.psum_scatter(
        lax.dot_general(
            back_slope, pooled, (((0,), (0,)), ((), ())), preferred_element_type=jnp.float32
        ),
        "table",
        scatter_dimension=0,
        tiled=True,
    )


def local(
    table_rows,
    row_state,
    parity,
    parity_slot,
    row_shard,
    row_offset,
    labels,
    first_weight,
    last_weight,
):
    tables = lax.axis_size("table")
    feat_count = row_offset.shape[2]
    local_rows = table_rows.shape[1]
    per_feature = local_rows // feat_count
    row_width = table_rows.shape[2]
    batch_rows = row_offset.shape[1]
    lookups = batch_rows * feat_count
    capacity = 2 * lookups // tables
    target = row_shard.reshape(lookups)
    feat_idx = jnp.arange(feat_count, dtype=jnp.int32)
    local_index = (feat_idx[None, :] * per_feature + row_offset[0]).reshape(lookups)
    onehot = (target[:, None] == jnp.arange(tables, dtype=jnp.int32)[None, :]).astype(jnp.int32)
    rank_run = jnp.cumsum(onehot, axis=0) - 1
    slot_place = target * capacity + jnp.sum(rank_run * onehot, axis=1)
    requests = (
        jnp.full((tables * capacity,), -1, jnp.int32)
        .at[slot_place]
        .set(local_index)
        .reshape(tables, capacity)
    )
    own_rows = table_rows[0]
    wanted_rows = lax.all_to_all(requests, "table", split_axis=0, concat_axis=0, tiled=True)
    rows_out = own_rows[jnp.clip(wanted_rows, 0, local_rows - 1)].astype(jnp.bfloat16)
    returned = lax.all_to_all(rows_out, "table", split_axis=0, concat_axis=0, tiled=True)
    returned, wanted_rows = (returned, wanted_rows)
    pooled = returned.reshape(tables * capacity, row_width)[slot_place].reshape(
        batch_rows, feat_count * row_width
    )
    partial_value = jnp.dot(pooled, first_weight, preferred_element_type=jnp.float32)
    pre_act = lax.psum(partial_value, "group")
    back_slope = head_slope(pre_act, labels, last_weight)
    first_grad = weight_gradient(back_slope, pooled)
    pooled_grad = lax.dot_general(
        back_slope, first_weight, (((1,), (1,)), ((), ())), preferred_element_type=jnp.float32
    ).astype(jnp.bfloat16)
    outgoing = (
        jnp.zeros((tables * capacity, row_width), jnp.bfloat16)
        .at[slot_place]
        .set(pooled_grad.reshape(lookups, row_width))
        .reshape(tables, capacity, row_width)
    )
    incoming = lax.all_to_all(outgoing, "table", split_axis=0, concat_axis=0, tiled=True)
    segment = jnp.where(wanted_rows >= 0, wanted_rows, local_rows).reshape(tables * capacity)
    row_grad = jax.ops.segment_sum(
        incoming.reshape(tables * capacity, row_width).astype(jnp.float32),
        segment,
        num_segments=local_rows + 1,
    )[:local_rows]
    new_state = row_state[0] + jnp.mean(row_grad * row_grad, axis=-1)
    change = -LEARN_RATE * row_grad * lax.rsqrt(new_state)[:, None]
    new_rows = own_rows + change
    stripes = change.reshape(-1, 2, parity.shape[2], row_width).sum(axis=1)
    ordered = jnp.zeros_like(stripes).at[parity_slot[0]].set(stripes)
    arrived = lax.psum_scatter(
        ordered.astype(jnp.bfloat16), "group", scatter_dimension=0, tiled=True
    ).astype(jnp.float32)
    new_parity = parity[0] + arrived
    return (new_rows[None], new_state[None], new_parity[None], first_grad)


def solution(mesh):
    placed = (
        P("group", "table", None),
        P("group", "table"),
        P("table", "group", None, None),
        P("table", None),
        P("group", "table", None, None),
        P("group", "table", None),
        P("table"),
        P("group", None),
        P(),
    )
    return jax.shard_map(
        local,
        mesh=mesh,
        in_specs=placed,
        out_specs=(
            P("group", "table", None),
            P("group", "table"),
            P("table", "group", None, None),
            P("table", "group"),
        ),
        check_vma=False,
    )
```

profile of v0, /device:TPU:16, one launch (start us, length us, event | category | flops | bytes accessed | tf_op | source)
XLA Modules:
  0.0 842.4 jit_solution(10322060309556948046)
XLA Ops:
  7.2 0.0 copy-start.4
  7.2 0.8 broadcast_multiply_fusion
  8.0 0.9 copy.14
  8.9 0.1 eq.29
  9.0 0.1 eq.25
  9.1 0.1 copy.13
  9.3 0.2 mul.72
  9.5 0.1 add.98
  9.6 0.0 copy-done.4
  9.6 0.1 copy.16
  9.7 0.1 squeeze.16
  9.9 0.1 fusion.10
  10.0 9.5 %reduce-window.6 = s32[32,64,128]{2,1,0:T(8,128)S(1)} reduce-window(s32[32,64,128]{2,1,0:T(8,128)S(1)} %fusion.10, s32[]{:T(128)} %constant.16.clone.1), window={size=1x1x128 pad=0_0x0_0x127_0}, to_apply=%region_0.0 | reduce-window | flops 33292288 | bytes 2097156 | tf_op jit(solution)/shard_map/reduce-window
  19.5 0.9 slice_reduce_fusion
  20.4 0.0 copy-start
  20.5 0.2 reduce-window.9
  20.7 0.3 add_add_fusion
  21.0 0.8 fusion.8
  21.8 0.1 compare_select_fusion.2
  21.9 30.5 %scatter_custom_fusion = s32[16384]{0:T(1024)S(1)} fusion(s32[8192]{0:T(1024)S(1)} %bitcast.75, s32[8192]{0:T(1024)S(1)} %add.99, s32[]{:T(128)} %constant.14.clone.1), kind=kCustom, calls=%fused_computation.34 | custom fusion | bytes 65540 | tf_op jit(solution)/shard_map/scatter | solution.py:58
  52.4 18.1 %all_to_all.22 = s32[32,1,512]{2,1,0:T(1,128)S(1)} all-to-all(s32[32,1,512]{2,1,0:T(1,128)S(1)} %bitcast.72), channel_id=1, replica_groups=mesh['group'=8,'table'=32] {'table'}, dimensions={0} | all-to-all | bytes 131072 | tf_op jit(solution)/shard_map/all_to_all | solution.py:62
  70.4 0.1 compare_select_fusion
  70.6 0.0 copy-done
  70.6 54.9 %gather_fusion = bf16[16384,128]{1,0:T(8,128)(2,1)} fusion(f32[4096,128]{1,0:T(8,128)S(1)} %bitcast.66, s32[16384]{0:T(1024)S(1)} %broadcast_clamp_fusion), kind=kCustom, calls=%fused_computation | custom fusion | bytes 8454144 | tf_op jit(solution)/shard_map/gather | solution.py:63
  125.5 4.8 all-to-all-start.1
  130.3 0.2 all-reduce.2.cloned.1.call-start
  130.6 96.4 %all-to-all-done.1 = bf16[32,512,128]{2,1,0:T(8,128)(2,1)} async-done(((bf16[32,512,128]{2,1,0:T(8,128)(2,1)}), bf16[32,512,128]{2,1,0:T(8,128)(2,1)}, u32[]{:S(2)}, u32[]{:S(2)}) %all-to-all-start.1) | async-done | bytes 4194336 | tf_op jit(solution)/shard_map/all_to_all | solution.py:64
  227.0 31.0 %gather_fusion.1 = bf16[8192,128]{1,0:T(8,128)(2,1)} fusion(bf16[16384,128]{1,0:T(8,128)(2,1)} %bitcast.10, s32[8192]{0:T(1024)S(1)} %broadcast_clamp_fusion.1), kind=kCustom, calls=%fused_computation.1 | custom fusion | bytes 4227072 | tf_op jit(solution)/shard_map/gather | solution.py:66
  258.0 4.2 reshape.177
  262.2 6.5 fusion.17
  268.6 0.0 copy-start.8
  268.7 0.0 all-reduce.2.cloned.1.call-update
  268.7 106.3 %all-reduce.2.cloned.1.call-done = f32[512,1024]{1,0:T(8,128)} async-done(((f32[512,1024]{1,0:T(8,128)}), f32[512,1024]{1,0:T(8,128)}) %all-reduce.2.cloned.1.call-update) | async-done | bytes 2097168 | tf_op jit(solution)/shard_map/psum | solution.py:70
  374.9 0.0 copy-done.8
  374.9 4.0 fusion.2
  379.0 0.0 copy-done.5
  379.0 0.0 copy-done.6
  379.0 0.0 copy-done.7
  379.0 4.3 convolution_convert_fusion
  383.3 4.2 reshape.210
  387.5 23.9 %scatter_custom_fusion.1 = bf16[16384,128]{1,0:T(8,128)(2,1)} fusion(s32[8192]{0:T(1024)S(1)} %bitcast.77, bf16[8192,128]{1,0:T(8,128)(2,1)} %reshape.210, bf16[]{:T(256)} %constant.20.clone.1), kind=kCustom, calls=%fused_computation.15 | custom fusion | bytes 4194816 | tf_op jit(solution)/shard_map/scatter | solution.py:79
  411.5 7.7 all-to-all-start.2
  419.2 0.3 reduce-scatter.3.cloned.1.call-start
  419.4 0.0 copy-done.9
  419.4 0.1 compare_select_fusion.1
  419.5 96.3 %all-to-all-done.2 = bf16[32,512,128]{2,1,0:T(8,128)(2,1)} async-done(((bf16[32,512,128]{2,1,0:T(8,128)(2,1)}), bf16[32,512,128]{2,1,0:T(8,128)(2,1)}, u32[]{:S(2)}, u32[]{:S(2)}) %all-to-all-start.2) | async-done | bytes 4194336 | tf_op jit(solution)/shard_map/all_to_all | solution.py:82
  515.8 92.0 %scatter_custom_fusion.2 = f32[4097,128]{1,0:T(8,128)} fusion(s32[16384]{0:T(1024)S(1)} %bitcast.79, bf16[16384,128]{1,0:T(8,128)(2,1)} %bitcast.23, f32[]{:T(128)} %constant.13.clone.1), kind=kCustom, calls=%fused_computation.6 | custom fusion | flops 4194304 | bytes 6291972 | tf_op jit(solution)/shard_map/scatter-add | solution.py:84
  607.9 2.4 multiply_reduce_fusion
  610.2 0.0 copy-done.3
  610.3 0.0 copy-done.1
  610.3 2.4 add_bitcast_fusion
  612.6 1.9 reduce_sum.32
  614.5 0.1 broadcast_in_dim.41
  614.6 1.6 scatter_fusion
  616.2 0.9 convert_element_type.36
  617.1 0.0 reduce-scatter.3.cloned.1.call-update
  617.2 0.0 reduce-scatter.5.cloned.1.call-start
  617.2 8.2 fusion.16
  625.4 0.0 reduce-scatter.5.cloned.1.call-update
  625.4 0.6 add.106
  626.1 75.6 %reduce-scatter.3.cloned.1.call-done = bf16[4,64,128]{2,1,0:T(8,128)(2,1)} async-done(((bf16[32,64,128]{2,1,0:T(8,128)(2,1)}), bf16[4,64,128]{2,1,0:T(8,128)(2,1)}) %reduce-scatter.3.cloned.1.call-update) | async-done | bytes 65552 | tf_op jit(solution)/shard_map/reduce_scatter | solution.py:94
  701.7 0.0 copy-done.2
  701.7 1.5 fusion.11
  703.2 132.7 %reduce-scatter.5.cloned.1.call-done = f32[32,2048]{1,0:T(8,128)} async-done(((f32[1024,2048]{1,0:T(8,128)}), f32[32,2048]{1,0:T(8,128)}) %reduce-scatter.5.cloned.1.call-update) | async-done | bytes 262160 | tf_op jit(solution)/shard_map/reduce_scatter | solution.py:20
  (15 shorter events, 0.1 us)
Async XLA Ops:
  7.2 2.4 copy-start.4
  20.4 50.1 %copy-start = (f32[1,4096,128]{2,1,0:T(8,128)S(1)}, f32[1,4096,128]{2,1,0:T(8,128)}, u32[]{:S(2)}) copy-start(f32[1,4096,128]{2,1,0:T(8,128)} %param.9) | copy-start | bytes 6291460
  125.5 101.5 %all-to-all-start.1 = ((bf16[32,512,128]{2,1,0:T(8,128)(2,1)}), bf16[32,512,128]{2,1,0:T(8,128)(2,1)}, u32[]{:S(2)}, u32[]{:S(2)}) async-start(bf16[32,512,128]{2,1,0:T(8,128)(2,1)} %bitcast.67), calls=%async_computation.1 | async-start | bytes 8388608 | tf_op jit(solution)/shard_map/all_to_all | solution.py:64
  130.3 244.6 %all-reduce.2.cloned.1.call-start = ((), (), s32[]{:S(2)}) async-start(), calls=%async_computation.5 | async-start | bytes 4194304 | tf_op jit(solution)/shard_map/psum | solution.py:70
  268.6 106.3 %copy-start.8 = (f32[1024]{0:T(1024)S(1)}, f32[1024]{0:T(1024)}, u32[]{:S(2)}) copy-start(f32[1024]{0:T(1024)} %param.17) | copy-start | bytes 12292
  374.9 4.0 copy-start.5
  374.9 4.1 copy-start.6
  374.9 4.1 copy-start.7
  411.5 7.9 copy-start.9
  411.5 104.4 %all-to-all-start.2 = ((bf16[32,512,128]{2,1,0:T(8,128)(2,1)}), bf16[32,512,128]{2,1,0:T(8,128)(2,1)}, u32[]{:S(2)}, u32[]{:S(2)}) async-start(bf16[32,512,128]{2,1,0:T(8,128)(2,1)} %bitcast.68), calls=%async_computation.2 | async-start | bytes 8388608 | tf_op jit(solution)/shard_map/all_to_all | solution.py:82
  419.2 282.5 %reduce-scatter.3.cloned.1.call-start = ((), (), s32[]{:S(2)}) async-start(), calls=%async_computation.6 | async-start | bytes 589824 | tf_op jit(solution)/shard_map/reduce_scatter | solution.py:94
  515.8 94.4 %copy-start.3 = (f32[1,4096]{1,0:T(1,128)S(1)}, f32[1,4096]{1,0:T(1,128)}, u32[]{:S(2)}) copy-start(f32[1,4096]{1,0:T(1,128)} %param.10) | copy-start | bytes 49156
  607.9 2.4 copy-start.1
  617.2 218.7 %reduce-scatter.5.cloned.1.call-start = ((), (), s32[]{:S(2)}) async-start(), calls=%async_computation.7 | async-start | bytes 8650752 | tf_op jit(solution)/shard_map/reduce_scatter | solution.py:20
  625.4 76.3 %copy-start.2 = (f32[1,4,64,128]{3,2,1,0:T(8,128)S(1)}, f32[1,4,64,128]{3,2,1,0:T(8,128)}, u32[]{:S(2)}) copy-start(f32[1,4,64,128]{3,2,1,0:T(8,128)} %param.11) | copy-start | bytes 393220
Sparse Core Ops, SparseCore 0:
  268.8 106.0 all-reduce.1
  617.3 84.3 reduce-scatter.2
  705.0 130.8 reduce-scatter.4
where the time goes:
time: 844 us; the launch traced here: 842 us
  waiting for transfers between devices  507 us (60%)
  local copies, waits for them, and re-layouts  153 us (18%)
  other arithmetic  114 us (14%)
  matrix products  23 us (3%)
  blocking collectives  18.1 us (2%)
  between operations  14.1 us (2%)
  starting transfers between devices  13 us (2%)
    reduce_scatter x1, waiting for transfers between devices, weight_gradient(): lax.psum_scatter(lax.dot_general(back_slope, pooled, (((0,), (0,)), ((),...  133 us
    psum x1, waiting for transfers between devices, local(): pre_act = lax.psum(partial_value, 'group')  106 us
    all_to_all x1, waiting for transfers between devices, local(): lax.all_to_all(rows_out, 'table', split_axis=0, concat_axis=0, tiled=True)  96.4 us
    all_to_all x1, waiting for transfers between devices, local(): lax.all_to_all(outgoing, 'table', split_axis=0, concat_axis=0, tiled=True)  96.3 us
    scatter-add x1, other arithmetic, local(): jax.ops.segment_sum(incoming.reshape(tables * capacity, row_width).astype...  92 us
    reduce_scatter x1, waiting for transfers between devices, local(): lax.psum_scatter(ordered.astype(jnp.bfloat16), 'group', scatter_dimension...  75.6 us
    gather x1, local copies, waits for them, and re-layouts, local(): own_rows[jnp.clip(wanted_rows, 0, local_rows - 1)].astype(jnp.bfloat16)  54.9 us
    gather x1, local copies, waits for them, and re-layouts, local(): returned.reshape(tables * capacity, row_width)[slot_place]  31 us
  transfers between devices with their start and end apart: 5, of which 5 were waited for; matrix products, arithmetic and copies ran while one was open for 1% of the time, Pallas kernels for 0%

commit v1 on v0

v1 whole, which is shorter than its diff:
```python
import functools

import jax
import jax.numpy as jnp
from jax import lax
from jax.experimental import pallas as pl
from jax.experimental.pallas import tpu as pltpu
from jax.sharding import PartitionSpec as P

LEARN_RATE = 0.1
TABLES = 32
CAP = 512
FEATS = 16
BATCH = 512
ROWS = 4096
PER_FEATURE = 256
WIDTH = 128
HIDDEN = 1024
LANES = 128
GROUP_OF = 16
ACCS = 8
VMEM_BYTES = 56 * 2**20

f32 = jnp.float32
bf16 = jnp.bfloat16
i32 = jnp.int32


def params():
    return pltpu.CompilerParams(vmem_limit_bytes=VMEM_BYTES)


def vmem():
    return pl.BlockSpec(memory_space=pltpu.VMEM)


def smem():
    return pl.BlockSpec(memory_space=pltpu.SMEM)


def dot_nt(a, b):
    return lax.dot_general(a, b, (((1,), (1,)), ((), ())), preferred_element_type=f32)


def iota(shape, axis):
    return lax.broadcasted_iota(i32, shape, axis)


def place_kernel(target_ref, offset_ref, slot_ref, request_ref, source_ref, rank_ref):
    chunks = BATCH // LANES
    lines = chunks * FEATS
    target = jnp.concatenate([target_ref[:, c * LANES : (c + 1) * LANES] for c in range(chunks)], axis=0)
    row, col = iota((LANES, LANES), 0), iota((LANES, LANES), 1)
    before = (row < col).astype(f32).astype(bf16)
    counter = jnp.concatenate([before, jnp.ones((LANES, LANES), bf16)], axis=1)
    earlier = (iota((lines, lines), 1) < iota((lines, lines), 0)).astype(f32).astype(bf16)
    rank = jnp.zeros((lines, LANES), f32)
    for t in range(TABLES):
        named = (target == t).astype(f32)
        counts = jnp.dot(named.astype(bf16), counter, preferred_element_type=f32)
        base = jnp.dot(earlier, counts[:, LANES:].astype(bf16), preferred_element_type=f32)
        rank = rank + named * (counts[:, :LANES] + base)
    rank = rank.astype(i32)
    rank = jnp.concatenate([rank[c * FEATS : (c + 1) * FEATS] for c in range(chunks)], axis=1)
    rank_ref[...] = rank
    slot_ref[...] = target_ref[...] * CAP + rank
    owner = iota((TABLES, BATCH), 0)
    sample = iota((TABLES, BATCH), 1)
    place = iota((CAP, BATCH), 0)

    def feature(f, total):
        named = target_ref[pl.ds(f, 1), :] == owner
        first = jnp.where(named, f + 1 + 32 * (sample // 256), 0)
        second = jnp.where(named, jnp.broadcast_to(offset_ref[pl.ds(f, 1), :], named.shape), 0)
        third = jnp.where(named, sample % 256, 0)
        values = jnp.concatenate([first, second, third], axis=0).astype(f32).astype(bf16)
        chosen = (rank_ref[pl.ds(f, 1), :] == place).astype(f32).astype(bf16)
        return total + dot_nt(values, chosen)

    total = lax.fori_loop(0, FEATS, feature, jnp.zeros((3 * TABLES, CAP), f32)).astype(i32)
    first, second, third = (total[k * TABLES : (k + 1) * TABLES] for k in range(3))
    used = first > 0
    f = first % 32 - 1
    request_ref[...] = jnp.where(used, f * PER_FEATURE + second, -1)
    source_ref[...] = jnp.where(used, f * BATCH + (first // 32) * 256 + third, 0)


def place(target, offset):
    return pl.pallas_call(
        place_kernel,
        out_shape=(
            jax.ShapeDtypeStruct((FEATS, BATCH), i32),
            jax.ShapeDtypeStruct((TABLES, CAP), i32),
            jax.ShapeDtypeStruct((TABLES, CAP), i32),
        ),
        in_specs=[vmem()] * 2,
        out_specs=(vmem(),) * 3,
        scratch_shapes=[pltpu.VMEM((FEATS, BATCH), i32)],
        compiler_params=params(),
        name="place",
    )(target, offset)


def pick_rows(count, index_ref, start, table_ref, block_ref):
    def group(k, carry):
        at = pl.multiple_of(k * GROUP_OF, GROUP_OF)
        for j in range(GROUP_OF):
            block_ref[pl.ds(at + j, 1), :] = table_ref[pl.ds(index_ref[start + at + j], 1), :]
        return carry

    lax.fori_loop(0, (count + GROUP_OF - 1) // GROUP_OF, group, 0)


def serve_kernel(index_ref, count_ref, table_ref, out_ref, block_ref):
    def peer(t, carry):
        pick_rows(count_ref[t], index_ref, t * CAP, table_ref, block_ref)
        out_ref[t] = block_ref[...].astype(bf16)
        return carry

    lax.fori_loop(0, TABLES, peer, 0)


def serve(index, count, table):
    return pl.pallas_call(
        serve_kernel,
        out_shape=jax.ShapeDtypeStruct((TABLES, CAP, WIDTH), bf16),
        in_specs=[smem(), smem(), vmem()],
        out_specs=vmem(),
        scratch_shapes=[pltpu.VMEM((CAP, WIDTH), f32)],
        compiler_params=params(),
        name="serve",
    )(index, count, table)


def forward_kernel(slot_ref, returned_ref, weight_ref, pooled_ref, sum_ref, rows_ref, block_ref):
    def widen(t, carry):
        rows_ref[pl.ds(pl.multiple_of(t * CAP, CAP), CAP), :] = returned_ref[t].astype(f32)
        return carry

    lax.fori_loop(0, TABLES, widen, 0)
    for f in range(FEATS):
        pick_rows(BATCH, slot_ref, f * BATCH, rows_ref, block_ref)
        pooled_ref[:, f * WIDTH : (f + 1) * WIDTH] = block_ref[...].astype(bf16)

    def tile(m, carry):
        at = pl.ds(pl.multiple_of(m * 128, 128), 128)
        sum_ref[at, :] = jnp.dot(pooled_ref[at, :], weight_ref[...], preferred_element_type=f32)
        return carry

    lax.fori_loop(0, BATCH // 128, tile, 0)


def forward(slot, returned, weight):
    return pl.pallas_call(
        forward_kernel,
        out_shape=(
            jax.ShapeDtypeStruct((BATCH, FEATS * WIDTH), bf16),
            jax.ShapeDtypeStruct((BATCH, HIDDEN), f32),
        ),
        in_specs=[smem(), vmem(), vmem()],
        out_specs=(vmem(), vmem()),
        scratch_shapes=[pltpu.VMEM((TABLES * CAP, WIDTH), f32), pltpu.VMEM((BATCH, WIDTH), f32)],
        compiler_params=params(),
        name="forward",
    )(slot, returned, weight)


def backward_kernel(source_ref, count_ref, slope_ref, weight_ref, out_ref, rows_ref, block_ref):
    def pair(k, carry):
        at = pl.multiple_of(k * 2 * WIDTH, 2 * WIDTH)
        both = dot_nt(slope_ref[...], weight_ref[pl.ds(at, 2 * WIDTH), :]).astype(bf16).astype(f32)
        to = pl.multiple_of(k * 2 * BATCH, 2 * BATCH)
        rows_ref[pl.ds(to, BATCH), :] = both[:, :WIDTH]
        rows_ref[pl.ds(to + BATCH, BATCH), :] = both[:, WIDTH:]
        return carry

    lax.fori_loop(0, FEATS // 2, pair, 0)

    def peer(t, carry):
        pick_rows(count_ref[t], source_ref, t * CAP, rows_ref, block_ref)
        out_ref[t] = block_ref[...].astype(bf16)
        return carry

    lax.fori_loop(0, TABLES, peer, 0)


def backward(source, count, slope, weight):
    return pl.pallas_call(
        backward_kernel,
        out_shape=jax.ShapeDtypeStruct((TABLES, CAP, WIDTH), bf16),
        in_specs=[smem(), smem(), vmem(), vmem()],
        out_specs=vmem(),
        scratch_shapes=[pltpu.VMEM((FEATS * BATCH, WIDTH), f32), pltpu.VMEM((CAP, WIDTH), f32)],
        compiler_params=params(),
        name="backward",
    )(source, count, slope, weight)


def update_kernel(
    index_ref, count_ref, slot_ref, incoming_ref, table_ref, state_ref, rows_ref, new_state_ref, stripes_ref, block_ref, *accs
):
    def clear(k, carry):
        at = pl.ds(pl.multiple_of(k * 128, 128), 128)
        for acc in accs:
            acc[at, :] = jnp.zeros((128, WIDTH), f32)
        return carry

    lax.fori_loop(0, ROWS // 128, clear, 0)

    def peer(t, carry):
        block_ref[...] = incoming_ref[t].astype(f32)

        def group(k, inner):
            at = pl.multiple_of(k * ACCS, ACCS)
            for j in range(ACCS):
                row = index_ref[t * CAP + at + j]
                accs[j][pl.ds(row, 1), :] = accs[j][pl.ds(row, 1), :] + block_ref[pl.ds(at + j, 1), :]
            return inner

        return lax.fori_loop(0, (count_ref[t] + ACCS - 1) // ACCS, group, carry)

    lax.fori_loop(0, TABLES, peer, 0)
    half = WIDTH // 2
    same = iota((WIDTH, WIDTH), 0) == iota((WIDTH, WIDTH), 1)

    def stripe(s, carry):
        at = pl.ds(pl.multiple_of(s * 128, 128), 128)
        grad = accs[0][at, :]
        for acc in accs[1:]:
            grad = grad + acc[at, :]
        mean = jnp.sum(grad * grad, axis=1, keepdims=True) * (1.0 / WIDTH)
        state = jnp.sum(jnp.where(same, state_ref[pl.ds(s, 1), :], 0.0), axis=1, keepdims=True) + mean
        change = -LEARN_RATE * grad * lax.rsqrt(state)
        rows_ref[at, :] = table_ref[at, :] + change
        new_state_ref[pl.ds(s, 1), :] = jnp.sum(jnp.where(same, state, 0.0), axis=0, keepdims=True)
        stripes_ref[slot_ref[s]] = (change[:half] + change[half:]).astype(bf16)
        return carry

    lax.fori_loop(0, ROWS // 128, stripe, 0)


def update(index, count, slot, incoming, table, state):
    return pl.pallas_call(
        update_kernel,
        out_shape=(
            jax.ShapeDtypeStruct((ROWS, WIDTH), f32),
            jax.ShapeDtypeStruct((ROWS // WIDTH, WIDTH), f32),
            jax.ShapeDtypeStruct((ROWS // WIDTH, WIDTH // 2, WIDTH), bf16),
        ),
        in_specs=[smem(), smem(), smem(), vmem(), vmem(), vmem()],
        out_specs=(vmem(),) * 3,
        scratch_shapes=[pltpu.VMEM((CAP, WIDTH), f32)] + [pltpu.VMEM((ROWS + 8, WIDTH), f32)] * ACCS,
        compiler_params=params(),
        name="update",
    )(index, count, slot, incoming, table, state)


def head_slope(pre_act, label_rows, last_weight):
    activated = jax.nn.silu(pre_act)
    logits = jnp.dot(activated, last_weight, precision=lax.Precision.HIGHEST)
    residual = jax.nn.sigmoid(logits) - label_rows.astype(f32)
    sig_pre = jax.nn.sigmoid(pre_act)
    return (residual[:, None] * last_weight[None, :] * (sig_pre * (1.0 + pre_act * (1.0 - sig_pre)))).astype(bf16)


def local(
    table_rows,
    row_state,
    parity,
    parity_slot,
    row_shard,
    row_offset,
    labels,
    first_weight,
    last_weight,
):
    table = table_rows[0]
    target = jnp.transpose(row_shard[0, :, :, 0])
    offset = jnp.transpose(row_offset[0])
    slot, request, source = place(target, offset)
    sent = jnp.sum((request >= 0).astype(i32), axis=1)
    wanted = lax.all_to_all(request, "table", split_axis=0, concat_axis=0, tiled=True)
    served = jnp.sum((wanted >= 0).astype(i32), axis=1)
    rows_out = serve(jnp.maximum(wanted, 0).reshape(-1), served, table)
    returned = lax.all_to_all(rows_out, "table", split_axis=0, concat_axis=0, tiled=True)
    pooled, partial_sum = forward(slot.reshape(-1), returned, first_weight)
    share = lax.psum_scatter(partial_sum, "group", scatter_dimension=0, tiled=True)
    samples = share.shape[0]
    own = lax.dynamic_slice(labels, (lax.axis_index("group") * samples,), (samples,))
    slope = lax.all_gather(head_slope(share, own, last_weight), "group", axis=0, tiled=True)
    weight_grad = lax.dot_general(slope, pooled, (((0,), (0,)), ((), ())), preferred_element_type=f32)
    slope, weight_grad = lax.optimization_barrier((slope, weight_grad))
    first_grad = lax.psum_scatter(weight_grad, "table", scatter_dimension=0, tiled=True)
    outgoing = backward(source.reshape(-1), sent, slope, first_weight)
    incoming = lax.all_to_all(outgoing, "table", split_axis=0, concat_axis=0, tiled=True)
    segment = jnp.where(wanted >= 0, wanted, ROWS).reshape(-1)
    new_rows, new_state, stripes = update(
        segment, served, parity_slot[0], incoming, table, row_state.reshape(ROWS // WIDTH, WIDTH)
    )
    arrived = lax.psum_scatter(stripes, "group", scatter_dimension=0, tiled=True).astype(f32)
    new_parity = parity[0] + arrived
    return (new_rows[None], new_state.reshape(1, ROWS), new_parity[None], first_grad)


def solution(mesh):
    placed = (
        P("group", "table", None),
        P("group", "table"),
        P("table", "group", None, None),
        P("table", None),
        P("group", "table", None, None),
        P("group", "table", None),
        P("table"),
        P("group", None),
        P(),
    )
    return jax.shard_map(
        local,
        mesh=mesh,
        in_specs=placed,
        out_specs=(
            P("group", "table", None),
            P("group", "table"),
            P("table", "group", None, None),
            P("table", "group"),
        ),
        check_vma=False,
    )
```

time: 844 us -> 681 us (0.81)
  local copies, waits for them, and re-layouts: 153 us -> 3.57 us
  other arithmetic: 114 us -> 5.85 us
  blocking collectives: 18.1 us -> 122 us
  Pallas kernels: 0 us -> 76.4 us
  waiting for transfers between devices: 507 us -> 436 us
  matrix products: 23 us -> 8.81 us
    psum x1 -> x0, waiting for transfers between devices: 106 us -> none  [local(): pre_act = lax.psum(partial_value, 'group')]
    all_to_all x1 -> x2, blocking collectives: 18.1 us -> 122 us  [the longest x1 104 us: local(): lax.all_to_all(outgoing, 'table', split_axis=0, concat_axis=0, tiled=True)]
    all_to_all x1 -> x0, waiting for transfers between devices: 96.3 us -> none  [local(): lax.all_to_all(outgoing, 'table', split_axis=0, concat_axis=0, tiled=True)]
    scatter-add x1 -> x0, other arithmetic: 92 us -> none  [local(): jax.ops.segment_sum(incoming.reshape(tables * capacity, row_width).astype...]
    gather x2 -> x0, local copies, waits for them, and re-layouts: 85.9 us -> none  [the longest x1 54.9 us: local(): own_rows[jnp.clip(wanted_rows, 0, local_rows - 1)].astype(jnp.bfloat16)]
    reduce_scatter x2 -> x3, waiting for transfers between devices: 208 us -> 290 us  [the longest x1 133 us: local(): lax.psum_scatter(weight_grad, 'table', scatter_dimension=0, tiled=True)]
    pallas_call x0 -> x5, Pallas kernels: none -> 76.4 us  [the longest x1 19.8 us: update(): pl.pallas_call(update_kernel, out_shape=(jax.ShapeDtypeStruct((ROWS, WIDT...]
    scatter x3 -> x0, local copies, waits for them, and re-layouts: 56 us -> none  [the longest x1 30.5 us: local(): requests = jnp.full((tables * capacity,), -1, jnp.int32).at[slot_place].s...]
where the time goes in v1:
time: 681 us; the launch traced here: 680 us
  waiting for transfers between devices  436 us (64%)
  blocking collectives  122 us (18%)
  Pallas kernels  76.4 us (11%)
  between operations  13.8 us (2%)
  starting transfers between devices  13.4 us (2%)
  matrix products  8.81 us (1%)
    reduce_scatter x1, waiting for transfers between devices, local(): lax.psum_scatter(weight_grad, 'table', scatter_dimension=0, tiled=True)  133 us
    all_to_all x1, blocking collectives, local(): lax.all_to_all(outgoing, 'table', split_axis=0, concat_axis=0, tiled=True)  104 us
    all_to_all x1, waiting for transfers between devices, local(): lax.all_to_all(rows_out, 'table', split_axis=0, concat_axis=0, tiled=True)  96 us
    reduce_scatter x1, waiting for transfers between devices, local(): lax.psum_scatter(stripes, 'group', scatter_dimension=0, tiled=True)  82.9 us
    reduce_scatter x1, waiting for transfers between devices, local(): lax.psum_scatter(partial_sum, 'group', scatter_dimension=0, tiled=True)  74.6 us
    all_gather x1, waiting for transfers between devices, local(): lax.all_gather(head_slope(share, own, last_weight), 'group', axis=0, tile...  49.1 us
    pallas_call x1, Pallas kernels, update(): pl.pallas_call(update_kernel, out_shape=(jax.ShapeDtypeStruct((ROWS, WIDT...  19.8 us
    pallas_call x1, Pallas kernels, backward(): pl.pallas_call(backward_kernel, out_shape=jax.ShapeDtypeStruct((TABLES, C...  18.1 us
  transfers between devices with their start and end apart: 5, of which 5 were waited for; matrix products, arithmetic and copies ran while one was open for 1% of the time, Pallas kernels for 0%

profile of v1, /device:TPU:16, one launch (start us, length us, event | category | flops | bytes accessed | tf_op | source)
XLA Modules:
  0.0 679.9 jit_solution(14701571623681868176)
XLA Ops:
  7.2 1.4 copy.18
  8.5 9.2 %place.1 = (s32[16,512]{1,0:T(8,128)}, s32[32,512]{1,0:T(8,128)}, s32[32,512]{1,0:T(8,128)}) custom-call(s32[16,512]{1,0:T(8,128)} %bitcast.47, s32[16,512]{1,0:T(8,128)} %bitcast.49), custom_call_target="tpu_custom_call" | custom-call | tf_op jit(solution)/shard_map/place/pallas_call | solution.py:89
  17.8 0.9 copy.13
  18.7 18.1 %all_to_all.22 = s32[32,1,512]{2,1,0:T(1,128)S(1)} all-to-all(s32[32,1,512]{2,1,0:T(1,128)S(1)} %copy.13), channel_id=1, replica_groups=mesh['group'=8,'table'=32] {'table'}, dimensions={0} | all-to-all | bytes 131072 | tf_op jit(solution)/shard_map/all_to_all | solution.py:282
  36.7 0.7 broadcast_maximum_fusion
  37.4 1.3 fusion.8.count_ref
  38.7 11.6 %serve.1 = bf16[32,512,128]{2,1,0:T(8,128)(2,1)} custom-call(s32[16384]{0:T(1024)} %get-tuple-element.24.index_ref, s32[32]{0:T(128)} %fusion.8.count_ref, f32[4096,128]{1,0:T(8,128)} %bitcast.41), custom_call_target="tpu_custom_call" | custom-call | tf_op jit(solution)/shard_map/serve/pallas_call | solution.py:124
  50.3 0.0 copy-start.3
  50.3 13.2 %all-to-all-start.1 = ((bf16[32,512,128]{2,1,0:T(8,128)(2,1)}), bf16[32,512,128]{2,1,0:T(8,128)(2,1)}, u32[]{:S(2)}, u32[]{:S(2)}) async-start(bf16[32,512,128]{2,1,0:T(8,128)(2,1)} %serve.1), calls=%async_computation.1 | async-start | bytes 8388608 | tf_op jit(solution)/shard_map/all_to_all | solution.py:285
  63.5 0.0 reduce-scatter.4.cloned.1.call-start
  63.6 0.0 copy-done.3
  63.6 0.6 copy.16
  64.2 96.0 %all-to-all-done.1.returned_ref = bf16[32,512,128]{2,1,0:T(8,128)(2,1)} async-done(((bf16[32,512,128]{2,1,0:T(8,128)(2,1)}), bf16[32,512,128]{2,1,0:T(8,128)(2,1)}, u32[]{:S(2)}, u32[]{:S(2)}) %all-to-all-start.1) | async-done | bytes 4194336 | tf_op jit(solution)/shard_map/all_to_all | solution.py:285
  160.2 0.0 copy-start.4
  160.2 0.0 copy-start.2
  160.2 0.0 copy-start
  160.2 17.7 %forward.1 = (bf16[512,2048]{1,0:T(8,128)(2,1)}, f32[512,1024]{1,0:T(8,128)}) custom-call(s32[8192]{0:T(1024)} %bitcast.46, bf16[32,512,128]{2,1,0:T(8,128)(2,1)} %all-to-all-done.1.returned_ref, bf16[2048,1024]{1,0:T(8,128)(2,1)} %weight_ref.3), custom_call_target="tpu_custom_call" | custom-call | tf_op jit(solution)/shard_map/forward/pallas_call | solution.py:154
  177.9 0.0 reduce-scatter.4.cloned.1.call-update
  177.9 0.0 all-gather.2.cloned.1.call-start
  178.0 74.6 %reduce-scatter.4.cloned.1.call-done = f32[64,1024]{1,0:T(8,128)} async-done(((f32[512,1024]{1,0:T(8,128)}), f32[64,1024]{1,0:T(8,128)}) %reduce-scatter.4.cloned.1.call-update) | async-done | bytes 262160 | tf_op jit(solution)/shard_map/reduce_scatter | solution.py:287
  252.6 0.0 copy-done.4
  252.6 1.3 fusion.4
  253.9 1.8 multiply_convert_fusion
  255.7 0.0 all-gather.2.cloned.1.call-update
  255.7 0.0 reduce-scatter.6.cloned.1.call-start
  255.8 0.0 copy-done.2
  255.8 0.6 copy.15
  256.4 0.0 copy-done
  256.4 0.6 convert_reduce_fusion.count_ref
  257.0 49.1 %all-gather.2.cloned.1.call-done.slope_ref = bf16[512,1024]{1,0:T(8,128)(2,1)} async-done(((bf16[64,1024]{1,0:T(8,128)(2,1)}), bf16[512,1024]{1,0:T(8,128)(2,1)}) %all-gather.2.cloned.1.call-update) | async-done | bytes 1048592 | tf_op jit(solution)/shard_map/all_gather | solution.py:290
  306.1 7.5 %fusion.10 = f32[1024,2048]{1,0:T(8,128)} fusion(bf16[512,1024]{1,0:T(8,128)(2,1)} %all-gather.2.cloned.1.call-done.slope_ref, bf16[512,2048]{1,0:T(8,128)(2,1)} %get-tuple-element.18), kind=kOutput, calls=%fused_computation.19 | convolution fusion | flops 2147483648 | bytes 11534336 | tf_op jit(solution)/shard_map/dot_general | solution.py:291
  313.6 18.1 %backward.1 = bf16[32,512,128]{2,1,0:T(8,128)(2,1)} custom-call(s32[16384]{0:T(1024)} %bitcast.44, s32[32]{0:T(128)} %convert_reduce_fusion.count_ref, bf16[512,1024]{1,0:T(8,128)(2,1)} %all-gather.2.cloned.1.call-done.slope_ref, bf16[2048,1024]{1,0:T(8,128)(2,1)} %weight_ref.3), custom_call_target="tpu_custom_call" | custom-call | tf_op jit(solution)/shard_map/backward/pallas_call | solution.py:188
  331.7 103.9 %all_to_all.23.incoming_ref = bf16[32,512,128]{2,1,0:T(8,128)(2,1)} all-to-all(bf16[32,512,128]{2,1,0:T(8,128)(2,1)} %backward.1), channel_id=1, replica_groups=mesh['group'=8,'table'=32] {'table'}, dimensions={0} | all-to-all | bytes 8388608 | tf_op jit(solution)/shard_map/all_to_all | solution.py:295
  435.6 19.8 %update.1 = (f32[4096,128]{1,0:T(8,128)}, f32[32,128]{1,0:T(8,128)}, bf16[32,64,128]{2,1,0:T(8,128)(2,1)}) custom-call(s32[16384]{0:T(1024)} %get-tuple-element.25.index_ref, s32[32]{0:T(128)} %fusion.8.count_ref, s32[32]{0:T(128)} %bitcast.53, bf16[32,512,128]{2,1,0:T(8,128)(2,1)} %all_to_all.23.incoming_ref, f32[4096,128]{1,0:T(8,128)} %bitcast.42, ...), custom_call_target="tpu_custom_call" | custom-call | tf_op jit(solution)/shard_map/update/pallas_call | solution.py:243
  455.4 0.0 reduce-scatter.6.cloned.1.call-update
  455.4 0.0 copy-start.1
  455.4 0.0 reduce-scatter.8.cloned.1.call-start
  455.5 0.5 reduce-scatter.8.cloned.1.call-update
  456.0 82.9 %reduce-scatter.6.cloned.1.call-done = bf16[4,64,128]{2,1,0:T(8,128)(2,1)} async-done(((bf16[32,64,128]{2,1,0:T(8,128)(2,1)}), bf16[4,64,128]{2,1,0:T(8,128)(2,1)}) %reduce-scatter.6.cloned.1.call-update) | async-done | bytes 65552 | tf_op jit(solution)/shard_map/reduce_scatter | solution.py:300
  538.9 0.0 copy-done.1
  538.9 1.5 fusion.6
  540.5 132.9 %reduce-scatter.8.cloned.1.call-done = f32[32,2048]{1,0:T(8,128)} async-done(((f32[1024,2048]{1,0:T(8,128)}), f32[32,2048]{1,0:T(8,128)}) %reduce-scatter.8.cloned.1.call-update) | async-done | bytes 262160 | tf_op jit(solution)/shard_map/reduce_scatter | solution.py:293
Async XLA Ops:
  50.3 13.3 %copy-start.3 = (s32[16,512]{1,0:T(8,128)S(1)}, s32[16,512]{1,0:T(8,128)}, u32[]{:S(2)}) copy-start(s32[16,512]{1,0:T(8,128)} %get-tuple-element.16) | copy-start | bytes 98308
  50.3 109.9 %all-to-all-start.1 = ((bf16[32,512,128]{2,1,0:T(8,128)(2,1)}), bf16[32,512,128]{2,1,0:T(8,128)(2,1)}, u32[]{:S(2)}, u32[]{:S(2)}) async-start(bf16[32,512,128]{2,1,0:T(8,128)(2,1)} %serve.1), calls=%async_computation.1 | async-start | bytes 8388608 | tf_op jit(solution)/shard_map/all_to_all | solution.py:285
  63.5 189.1 %reduce-scatter.4.cloned.1.call-start = ((), (), s32[]{:S(2)}) async-start(), calls=%async_computation.6 | async-start | bytes 2359296 | tf_op jit(solution)/shard_map/reduce_scatter | solution.py:287
  160.2 92.4 %copy-start.4 = (f32[1024]{0:T(1024)S(1)}, f32[1024]{0:T(1024)}, u32[]{:S(2)}) copy-start(f32[1024]{0:T(1024)} %param.17) | copy-start | bytes 12292
  160.2 95.5 %copy-start.2 = (s32[32,512]{1,0:T(8,128)S(1)}, s32[32,512]{1,0:T(8,128)}, u32[]{:S(2)}) copy-start(s32[32,512]{1,0:T(8,128)} %get-tuple-element.15) | copy-start | bytes 196612
  160.2 96.2 %copy-start = (s32[32,512]{1,0:T(8,128)S(1)}, s32[32,512]{1,0:T(8,128)}, u32[]{:S(2)}) copy-start(s32[32,512]{1,0:T(8,128)} %get-tuple-element.14) | copy-start | bytes 196612
  177.9 128.1 %all-gather.2.cloned.1.call-start = ((), (), s32[]{:S(2)}) async-start(), calls=%async_computation.7 | async-start | bytes 1179648 | tf_op jit(solution)/shard_map/all_gather | solution.py:290
  255.7 283.2 %reduce-scatter.6.cloned.1.call-start = ((), (), s32[]{:S(2)}) async-start(), calls=%async_computation.8 | async-start | bytes 589824 | tf_op jit(solution)/shard_map/reduce_scatter | solution.py:300
  455.4 83.5 %copy-start.1 = (f32[1,4,64,128]{3,2,1,0:T(8,128)S(1)}, f32[1,4,64,128]{3,2,1,0:T(8,128)}, u32[]{:S(2)}) copy-start(f32[1,4,64,128]{3,2,1,0:T(8,128)} %param.11) | copy-start | bytes 393220
  455.4 217.9 %reduce-scatter.8.cloned.1.call-start = ((), (), s32[]{:S(2)}) async-start(), calls=%async_computation.9 | async-start | bytes 8650752 | tf_op jit(solution)/shard_map/reduce_scatter | solution.py:293
Sparse Core Ops, SparseCore 0:
  178.1 74.4 reduce-scatter.3
  255.8 50.2 all-gather.1
  455.6 83.3 reduce-scatter.5
  542.1 131.2 reduce-scatter.7

commit v2 on v1

--- a/solution.py
+++ b/solution.py
@@ -8,6 +8,7 @@
 from jax.sharding import PartitionSpec as P
 
 LEARN_RATE = 0.1
+GROUPS = 8
 TABLES = 32
 CAP = 512
 FEATS = 16
@@ -16,6 +17,8 @@
 PER_FEATURE = 256
 WIDTH = 128
 HIDDEN = 1024
+SHARE = BATCH // GROUPS
+OWNED = 32 // GROUPS
 LANES = 128
 GROUP_OF = 16
 ACCS = 8
@@ -24,10 +27,13 @@
 f32 = jnp.float32
 bf16 = jnp.bfloat16
 i32 = jnp.int32
-
-
-def params():
-    return pltpu.CompilerParams(vmem_limit_bytes=VMEM_BYTES)
+MESH = pl.DeviceIdType.MESH
+
+
+def params(collective_id=None):
+    if collective_id is None:
+        return pltpu.CompilerParams(vmem_limit_bytes=VMEM_BYTES)
+    return pltpu.CompilerParams(vmem_limit_bytes=VMEM_BYTES, collective_id=collective_id, has_side_effects=True)
 
 
 def vmem():
@@ -255,12 +261,94 @@
     )(index, count, slot, incoming, table, state)
 
 
-def head_slope(pre_act, label_rows, last_weight):
-    activated = jax.nn.silu(pre_act)
-    logits = jnp.dot(activated, last_weight, precision=lax.Precision.HIGHEST)
-    residual = jax.nn.sigmoid(logits) - label_rows.astype(f32)
+def greet(axis, size):
+    me = lax.axis_index(axis)
+    barrier = pltpu.get_barrier_semaphore()
+    for d in range(1, size):
+        pl.semaphore_signal(barrier, inc=1, device_id={axis: lax.rem(me + d, size)}, device_id_type=MESH)
+    pl.semaphore_wait(barrier, size - 1)
+
+
+def push(axis, peer, source, target, sent, got):
+    return pltpu.make_async_remote_copy(
+        src_ref=source, dst_ref=target, send_sem=sent, recv_sem=got, device_id={axis: peer}, device_id_type=MESH
+    )
+
+
+def mix_kernel(sum_ref, label_ref, last_ref, slope_ref, arrived_ref, sent, got, sent_slope, got_slope):
+    me = lax.axis_index("group")
+    greet("group", GROUPS)
+    copies = []
+    for d in range(1, GROUPS):
+        peer = lax.rem(me + d, GROUPS)
+        theirs = sum_ref.at[pl.ds(pl.multiple_of(peer * SHARE, SHARE), SHARE)]
+        copies.append(push("group", peer, theirs, arrived_ref.at[d], sent.at[d], got.at[d]))
+        copies[-1].start()
+    mine = pl.ds(pl.multiple_of(me * SHARE, SHARE), SHARE)
+    pre_act = sum_ref[mine, :]
+    for d in range(1, GROUPS):
+        copies[d - 1].wait_recv()
+        pre_act = pre_act + arrived_ref[d]
     sig_pre = jax.nn.sigmoid(pre_act)
-    return (residual[:, None] * last_weight[None, :] * (sig_pre * (1.0 + pre_act * (1.0 - sig_pre)))).astype(bf16)
+    last = last_ref[...]
+    logits = jnp.sum(pre_act * sig_pre * last, axis=1, keepdims=True)
+    residual = jax.nn.sigmoid(logits) - label_ref[...]
+    slope_ref[mine, :] = (residual * last * (sig_pre * (1.0 + pre_act * (1.0 - sig_pre)))).astype(bf16)
+    handed = []
+    for d in range(1, GROUPS):
+        peer = lax.rem(me + d, GROUPS)
+        handed.append(push("group", peer, slope_ref.at[mine], slope_ref.at[mine], sent_slope.at[d], got_slope.at[d]))
+        handed[-1].start()
+    for d in range(1, GROUPS):
+        copies[d - 1].wait_send()
+    for d in range(1, GROUPS):
+        handed[d - 1].wait_send()
+        them = pl.ds(pl.multiple_of(lax.rem(me + GROUPS - d, GROUPS) * SHARE, SHARE), SHARE)
+        theirs = slope_ref.at[them]
+        push("group", lax.rem(me + d, GROUPS), theirs, theirs, sent_slope.at[d], got_slope.at[d]).wait_recv()
+
+
+def mix(partial_sum, label, last):
+    return pl.pallas_call(
+        mix_kernel,
+        out_shape=jax.ShapeDtypeStruct((BATCH, HIDDEN), bf16),
+        in_specs=[vmem()] * 3,
+        out_specs=vmem(),
+        scratch_shapes=[pltpu.VMEM((GROUPS, SHARE, HIDDEN), f32)] + [pltpu.SemaphoreType.DMA((GROUPS,))] * 4,
+        compiler_params=params(0),
+        name="mix",
+    )(partial_sum, label, last)
+
+
+def stripe_kernel(stripes_ref, parity_ref, out_ref, arrived_ref, sent, got):
+    me = lax.axis_index("group")
+    greet("group", GROUPS)
+    copies = []
+    for d in range(1, GROUPS):
+        peer = lax.rem(me + d, GROUPS)
+        theirs = stripes_ref.at[pl.ds(peer * OWNED, OWNED)]
+        copies.append(push("group", peer, theirs, arrived_ref.at[d], sent.at[d], got.at[d]))
+        copies[-1].start()
+    total = stripes_ref[pl.ds(me * OWNED, OWNED)].astype(f32)
+    for copy in copies:
+        copy.wait_recv()
+    for d in range(1, GROUPS):
+        total = total + arrived_ref[d].astype(f32)
+    out_ref[...] = parity_ref[...] + total
+    for copy in copies:
+        copy.wait_send()
+
+
+def stripe_sum(stripes, parity):
+    return pl.pallas_call(
+        stripe_kernel,
+        out_shape=jax.ShapeDtypeStruct(parity.shape, f32),
+        in_specs=[vmem()] * 2,
+        out_specs=vmem(),
+        scratch_shapes=[pltpu.VMEM((GROUPS,) + parity.shape, bf16)] + [pltpu.SemaphoreType.DMA((GROUPS,))] * 2,
+        compiler_params=params(1),
+        name="stripe_sum",
+    )(stripes, parity)
 
 
 def local(
@@ -284,10 +372,8 @@
     rows_out = serve(jnp.maximum(wanted, 0).reshape(-1), served, table)
     returned = lax.all_to_all(rows_out, "table", split_axis=0, concat_axis=0, tiled=True)
     pooled, partial_sum = forward(slot.reshape(-1), returned, first_weight)
-    share = lax.psum_scatter(partial_sum, "group", scatter_dimension=0, tiled=True)
-    samples = share.shape[0]
-    own = lax.dynamic_slice(labels, (lax.axis_index("group") * samples,), (samples,))
-    slope = lax.all_gather(head_slope(share, own, last_weight), "group", axis=0, tiled=True)
+    own = lax.dynamic_slice(labels, (lax.axis_index("group") * SHARE,), (SHARE,)).astype(f32)
+    slope = mix(partial_sum, own[:, None], last_weight[None, :])
     weight_grad = lax.dot_general(slope, pooled, (((0,), (0,)), ((), ())), preferred_element_type=f32)
     slope, weight_grad = lax.optimization_barrier((slope, weight_grad))
     first_grad = lax.psum_scatter(weight_grad, "table", scatter_dimension=0, tiled=True)
@@ -297,8 +383,7 @@
     new_rows, new_state, stripes = update(
         segment, served, parity_slot[0], incoming, table, row_state.reshape(ROWS // WIDTH, WIDTH)
     )
-    arrived = lax.psum_scatter(stripes, "group", scatter_dimension=0, tiled=True).astype(f32)
-    new_parity = parity[0] + arrived
+    new_parity = stripe_sum(stripes, parity[0])
     return (new_rows[None], new_state.reshape(1, ROWS), new_parity[None], first_grad)
 
 

time: 681 us -> 425 us (0.62)
  waiting for transfers between devices: 436 us -> 102 us
  Pallas kernels: 76.4 us -> 141 us
  blocking collectives: 122 us -> 137 us
    reduce_scatter x2 -> x0, waiting for transfers between devices: 158 us -> none  [the longest x1 82.9 us: local(): lax.psum_scatter(stripes, 'group', scatter_dimension=0, tiled=True)]
    reduce_scatter x1, waiting for transfers between devices: 133 us -> 7.25 us  [local(): lax.psum_scatter(weight_grad, 'table', scatter_dimension=0, tiled=True)]
    pallas_call x0 -> x2, Pallas kernels: none -> 60.3 us  [the longest x1 43.4 us: mix(): pl.pallas_call(mix_kernel, out_shape=jax.ShapeDtypeStruct((BATCH, HIDDEN)...]
    all_gather x1 -> x0, waiting for transfers between devices: 49.1 us -> none  [local(): lax.all_gather(head_slope(share, own, last_weight), 'group', axis=0, tile...]
    all_to_all x1, blocking collectives: 104 us -> 119 us  [local(): lax.all_to_all(outgoing, 'table', split_axis=0, concat_axis=0, tiled=True)]
  transfers between devices with their start and end apart: 5 -> 2, of which waited for: 5 -> 2; matrix products, arithmetic and copies ran while one was open for 1% -> 1% of each run, Pallas kernels for 0% -> 14%
where the time goes in v2:
time: 425 us; the launch traced here: 422 us
  Pallas kernels  141 us (33%)
  blocking collectives  137 us (32%)
  waiting for transfers between devices  102 us (24%)
  between operations  14.1 us (3%)
  starting transfers between devices  10.7 us (3%)
  matrix products  7.53 us (2%)
  local copies, waits for them, and re-layouts  6.64 us (2%)
    all_to_all x1, blocking collectives, local(): lax.all_to_all(outgoing, 'table', split_axis=0, concat_axis=0, tiled=True)  119 us
    all_to_all x1, waiting for transfers between devices, local(): lax.all_to_all(rows_out, 'table', split_axis=0, concat_axis=0, tiled=True)  94.6 us
    pallas_call x1, Pallas kernels, mix(): pl.pallas_call(mix_kernel, out_shape=jax.ShapeDtypeStruct((BATCH, HIDDEN)...  43.4 us
    pallas_call x1, Pallas kernels, update(): pl.pallas_call(update_kernel, out_shape=(jax.ShapeDtypeStruct((ROWS, WIDT...  22.3 us
    all_to_all x1, blocking collectives, local(): lax.all_to_all(request, 'table', split_axis=0, concat_axis=0, tiled=True)  18.1 us
    pallas_call x1, Pallas kernels, backward(): pl.pallas_call(backward_kernel, out_shape=jax.ShapeDtypeStruct((TABLES, C...  18 us
    pallas_call x1, Pallas kernels, forward(): pl.pallas_call(forward_kernel, out_shape=(jax.ShapeDtypeStruct((BATCH, FE...  17.7 us
    pallas_call x1, Pallas kernels, stripe_sum(): pl.pallas_call(stripe_kernel, out_shape=jax.ShapeDtypeStruct(parity.shape...  16.9 us
  transfers between devices with their start and end apart: 2, of which 2 were waited for; matrix products, arithmetic and copies ran while one was open for 1% of the time, Pallas kernels for 14%

profile of v2, /device:TPU:16, one launch (start us, length us, event | category | flops | bytes accessed | tf_op | source)
XLA Modules:
  0.0 422.5 jit_solution(15152541794883160517)
XLA Ops:
  7.2 1.4 copy.20
  8.5 9.2 %place.1 = (s32[16,512]{1,0:T(8,128)}, s32[32,512]{1,0:T(8,128)}, s32[32,512]{1,0:T(8,128)}) custom-call(s32[16,512]{1,0:T(8,128)} %bitcast.33, s32[16,512]{1,0:T(8,128)} %bitcast.36), custom_call_target="tpu_custom_call" | custom-call | tf_op jit(solution)/shard_map/place/pallas_call | solution.py:95
  17.8 0.9 copy.14
  18.7 18.1 %all_to_all.22 = s32[32,1,512]{2,1,0:T(1,128)S(1)} all-to-all(s32[32,1,512]{2,1,0:T(1,128)S(1)} %copy.14), channel_id=1, replica_groups=mesh['group'=8,'table'=32] {'table'}, dimensions={0} | all-to-all | bytes 131072 | tf_op jit(solution)/shard_map/all_to_all | solution.py:370
  36.7 0.7 broadcast_maximum_fusion
  37.4 1.3 fusion.count_ref
  38.7 13.4 %serve.1 = bf16[32,512,128]{2,1,0:T(8,128)(2,1)} custom-call(s32[16384]{0:T(1024)} %get-tuple-element.24.index_ref, s32[32]{0:T(128)} %fusion.count_ref, f32[4096,128]{1,0:T(8,128)} %bitcast.26), custom_call_target="tpu_custom_call" | custom-call | tf_op jit(solution)/shard_map/serve/pallas_call | solution.py:130
  52.1 0.0 copy-start.2
  52.1 10.7 %all-to-all-start.1 = ((bf16[32,512,128]{2,1,0:T(8,128)(2,1)}), bf16[32,512,128]{2,1,0:T(8,128)(2,1)}, u32[]{:S(2)}, u32[]{:S(2)}) async-start(bf16[32,512,128]{2,1,0:T(8,128)(2,1)} %serve.1), calls=%async_computation.1 | async-start | bytes 8388608 | tf_op jit(solution)/shard_map/all_to_all | solution.py:373
  62.8 0.0 reduce-scatter.2.cloned.1.call-start
  62.8 0.8 convert_bitcast_fusion
  63.6 0.7 copy.15.label_ref
  64.3 0.0 copy-done.2
  64.3 0.6 copy.18
  64.9 94.6 %all-to-all-done.1.returned_ref = bf16[32,512,128]{2,1,0:T(8,128)(2,1)} async-done(((bf16[32,512,128]{2,1,0:T(8,128)(2,1)}), bf16[32,512,128]{2,1,0:T(8,128)(2,1)}, u32[]{:S(2)}, u32[]{:S(2)}) %all-to-all-start.1) | async-done | bytes 4194336 | tf_op jit(solution)/shard_map/all_to_all | solution.py:373
  159.5 17.7 %forward.1 = (bf16[512,2048]{1,0:T(8,128)(2,1)}, f32[512,1024]{1,0:T(8,128)}) custom-call(s32[8192]{0:T(1024)} %bitcast.32, bf16[32,512,128]{2,1,0:T(8,128)(2,1)} %all-to-all-done.1.returned_ref, bf16[2048,1024]{1,0:T(8,128)(2,1)} %weight_ref.3), custom_call_target="tpu_custom_call" | custom-call | tf_op jit(solution)/shard_map/forward/pallas_call | solution.py:160
  177.1 43.4 %mix.1.slope_ref = bf16[512,1024]{1,0:T(8,128)(2,1)} custom-call(f32[512,1024]{1,0:T(8,128)} %get-tuple-element.17.sum_ref, f32[64,1]{1,0:T(8,128)} %copy.15.label_ref, f32[1,1024]{1,0:T(1,128)} %bitcast.39), custom_call_target="tpu_custom_call" | custom-call | tf_op jit(solution)/shard_map/mix/pallas_call | solution.py:312
  220.5 7.5 %fusion.1 = f32[1024,2048]{1,0:T(8,128)} fusion(bf16[512,1024]{1,0:T(8,128)(2,1)} %mix.1.slope_ref, bf16[512,2048]{1,0:T(8,128)(2,1)} %get-tuple-element.18), kind=kOutput, calls=%fused_computation.7 | convolution fusion | flops 2147483648 | bytes 11534336 | tf_op jit(solution)/shard_map/dot_general | solution.py:377
  228.1 0.0 copy-start.1
  228.1 0.0 copy-start
  228.1 0.0 reduce-scatter.2.cloned.1.call-update
  228.1 0.8 copy-done.1
  228.9 0.6 copy.17
  229.6 0.0 copy-done
  229.6 0.6 convert_reduce_fusion.count_ref
  230.2 18.0 %backward.1 = bf16[32,512,128]{2,1,0:T(8,128)(2,1)} custom-call(s32[16384]{0:T(1024)} %bitcast.30, s32[32]{0:T(128)} %convert_reduce_fusion.count_ref, bf16[512,1024]{1,0:T(8,128)(2,1)} %mix.1.slope_ref, bf16[2048,1024]{1,0:T(8,128)(2,1)} %weight_ref.3), custom_call_target="tpu_custom_call" | custom-call | tf_op jit(solution)/shard_map/backward/pallas_call | solution.py:194
  248.2 119.4 %all_to_all.23.incoming_ref = bf16[32,512,128]{2,1,0:T(8,128)(2,1)} all-to-all(bf16[32,512,128]{2,1,0:T(8,128)(2,1)} %backward.1), channel_id=1, replica_groups=mesh['group'=8,'table'=32] {'table'}, dimensions={0} | all-to-all | bytes 8388608 | tf_op jit(solution)/shard_map/all_to_all | solution.py:381
  367.6 22.3 %update.1 = (f32[4096,128]{1,0:T(8,128)}, f32[32,128]{1,0:T(8,128)}, bf16[32,64,128]{2,1,0:T(8,128)(2,1)}) custom-call(s32[16384]{0:T(1024)} %get-tuple-element.25.index_ref, s32[32]{0:T(128)} %fusion.count_ref, s32[32]{0:T(128)} %bitcast.40, bf16[32,512,128]{2,1,0:T(8,128)(2,1)} %all_to_all.23.incoming_ref, f32[4096,128]{1,0:T(8,128)} %bitcast.27, ...), custom_call_target="tpu_custom_call" | custom-call | tf_op jit(solution)/shard_map/update/pallas_call | solution.py:249
  389.9 16.9 %stripe_sum.1 = f32[4,64,128]{2,1,0:T(8,128)} custom-call(bf16[32,64,128]{2,1,0:T(8,128)(2,1)} %get-tuple-element.22.stripes_ref, f32[4,64,128]{2,1,0:T(8,128)} %bitcast.34), custom_call_target="tpu_custom_call" | custom-call | tf_op jit(solution)/shard_map/stripe_sum/pallas_call | solution.py:343
  406.8 7.2 %reduce-scatter.2.cloned.1.call-done = f32[32,2048]{1,0:T(8,128)} async-done(((f32[1024,2048]{1,0:T(8,128)}), f32[32,2048]{1,0:T(8,128)}) %reduce-scatter.2.cloned.1.call-update) | async-done | bytes 262160 | tf_op jit(solution)/shard_map/reduce_scatter | solution.py:379
  414.1 1.6 copy.22
Async XLA Ops:
  52.1 12.2 %copy-start.2 = (s32[16,512]{1,0:T(8,128)S(1)}, s32[16,512]{1,0:T(8,128)}, u32[]{:S(2)}) copy-start(s32[16,512]{1,0:T(8,128)} %get-tuple-element.16) | copy-start | bytes 98308
  52.1 107.4 %all-to-all-start.1 = ((bf16[32,512,128]{2,1,0:T(8,128)(2,1)}), bf16[32,512,128]{2,1,0:T(8,128)(2,1)}, u32[]{:S(2)}, u32[]{:S(2)}) async-start(bf16[32,512,128]{2,1,0:T(8,128)(2,1)} %serve.1), calls=%async_computation.1 | async-start | bytes 8388608 | tf_op jit(solution)/shard_map/all_to_all | solution.py:373
  62.8 351.3 %reduce-scatter.2.cloned.1.call-start = ((), (), s32[]{:S(2)}) async-start(), calls=%async_computation.4 | async-start | bytes 8650752 | tf_op jit(solution)/shard_map/reduce_scatter | solution.py:379
  228.1 0.8 copy-start.1
  228.1 1.5 copy-start
Sparse Core Ops, SparseCore 0:
  228.2 185.8 reduce-scatter.1

commit v3 on v1

v3 whole, which is shorter than its diff:
```python
import functools

import jax
import jax.numpy as jnp
from jax import lax
from jax.experimental import pallas as pl
from jax.experimental.pallas import tpu as pltpu
from jax.sharding import PartitionSpec as P

LEARN_RATE = 0.1
GROUPS = 8
TABLES = 32
CAP = 512
FEATS = 16
BATCH = 512
ROWS = 4096
PER_FEATURE = 256
WIDTH = 128
HIDDEN = 1024
SHARE = BATCH // GROUPS
OWNED = 32 // GROUPS
LANES = 128
GROUP_OF = 16
ACCS = 8
VMEM_BYTES = 56 * 2**20

f32 = jnp.float32
bf16 = jnp.bfloat16
i32 = jnp.int32
MESH = pl.DeviceIdType.MESH


def params(collective_id=None):
    if collective_id is None:
        return pltpu.CompilerParams(vmem_limit_bytes=VMEM_BYTES)
    return pltpu.CompilerParams(vmem_limit_bytes=VMEM_BYTES, collective_id=collective_id, has_side_effects=True)


def vmem():
    return pl.BlockSpec(memory_space=pltpu.VMEM)


def smem():
    return pl.BlockSpec(memory_space=pltpu.SMEM)


def dot_nt(a, b):
    return lax.dot_general(a, b, (((1,), (1,)), ((), ())), preferred_element_type=f32)


def iota(shape, axis):
    return lax.broadcasted_iota(i32, shape, axis)


def hail(axis, size):
    me = lax.axis_index(axis)
    barrier = pltpu.get_barrier_semaphore()
    for d in range(1, size):
        pl.semaphore_signal(barrier, inc=1, device_id={axis: lax.rem(me + d, size)}, device_id_type=MESH)


def gather_in(size):
    pl.semaphore_wait(pltpu.get_barrier_semaphore(), size - 1)


def push(axis, peer, source, target, sent, got):
    return pltpu.make_async_remote_copy(
        src_ref=source, dst_ref=target, send_sem=sent, recv_sem=got, device_id={axis: peer}, device_id_type=MESH
    )


def dma(count):
    return pltpu.SemaphoreType.DMA((count,))


def place(target_ref, offset_ref, slot_ref, source_ref, request_ref, rank_ref):
    chunks = BATCH // LANES
    lines = chunks * FEATS
    target = jnp.concatenate([target_ref[:, c * LANES : (c + 1) * LANES] for c in range(chunks)], axis=0)
    row, col = iota((LANES, LANES), 0), iota((LANES, LANES), 1)
    before = (row < col).astype(f32).astype(bf16)
    counter = jnp.concatenate([before, jnp.ones((LANES, LANES), bf16)], axis=1)
    earlier = (iota((lines, lines), 1) < iota((lines, lines), 0)).astype(f32).astype(bf16)
    rank = jnp.zeros((lines, LANES), f32)
    for t in range(TABLES):
        named = (target == t).astype(f32)
        counts = jnp.dot(named.astype(bf16), counter, preferred_element_type=f32)
        base = jnp.dot(earlier, counts[:, LANES:].astype(bf16), preferred_element_type=f32)
        rank = rank + named * (counts[:, :LANES] + base)
    rank = rank.astype(i32)
    rank = jnp.concatenate([rank[c * FEATS : (c + 1) * FEATS] for c in range(chunks)], axis=1)
    rank_ref[...] = rank
    slot_ref[...] = target_ref[...] * CAP + rank
    owner = iota((TABLES, BATCH), 0)
    sample = iota((TABLES, BATCH), 1)
    spot = iota((CAP, BATCH), 0)

    def feature(f, total):
        named = target_ref[pl.ds(f, 1), :] == owner
        first = jnp.where(named, f + 1 + 32 * (sample // 256), 0)
        second = jnp.where(named, jnp.broadcast_to(offset_ref[pl.ds(f, 1), :], named.shape), 0)
        third = jnp.where(named, sample % 256, 0)
        values = jnp.concatenate([first, second, third], axis=0).astype(f32).astype(bf16)
        chosen = (rank_ref[pl.ds(f, 1), :] == spot).astype(f32).astype(bf16)
        return total + dot_nt(values, chosen)

    total = lax.fori_loop(0, FEATS, feature, jnp.zeros((3 * TABLES, CAP), f32)).astype(i32)
    first, second, third = (total[k * TABLES : (k + 1) * TABLES] for k in range(3))
    used = first > 0
    f = first % 32 - 1
    request = jnp.where(used, f * PER_FEATURE + second, -1)
    source = jnp.where(used, f * BATCH + (first // 32) * 256 + third, 0)
    for c in range(CAP // LANES):
        request_ref[:, c, :] = request[:, c * LANES : (c + 1) * LANES]
        source_ref[:, c, :] = source[:, c * LANES : (c + 1) * LANES]


def pick(index_ref, peer, table_ref, block_ref):
    for c in range(CAP // LANES):

        def group(k, carry):
            at = pl.multiple_of(k * GROUP_OF, GROUP_OF)
            for j in range(GROUP_OF):
                row = index_ref[peer, c, at + j]
                block_ref[pl.ds(c * LANES + at + j, 1), :] = table_ref[pl.ds(row, 1), :]
            return carry

        lax.fori_loop(0, LANES // GROUP_OF, group, 0)


def trade(me, index_ref, table_ref, block_ref, rows_ref, back_ref, sent, got):
    def serve(d, carry):
        peer = lax.rem(me + d, TABLES)
        pick(index_ref, peer, table_ref, block_ref)
        rows_ref[peer] = block_ref[...].astype(bf16)
        push("table", peer, rows_ref.at[peer], back_ref.at[me], sent.at[d], got.at[d]).start()
        return carry

    lax.fori_loop(1, TABLES, serve, 0)
    pick(index_ref, me, table_ref, block_ref)
    back_ref[me] = block_ref[...].astype(bf16)
    finish(me, rows_ref, back_ref, sent, got)


def finish(me, rows_ref, back_ref, sent, got):
    def settle(d, carry):
        peer = lax.rem(me + d, TABLES)
        giver = lax.rem(me + TABLES - d, TABLES)
        push("table", peer, rows_ref.at[peer], back_ref.at[giver], sent.at[d], got.at[d]).wait()
        return carry

    lax.fori_loop(1, TABLES, settle, 0)


def fetch_kernel(
    target_ref, offset_ref, table_ref, slot_ref, source_ref, wanted_ref, back_ref,
    rank_ref, request_ref, clip_ref, index_ref, block_ref, rows_ref, copied, sent_ask, got_ask, sent, got,
):
    me = lax.axis_index("table")
    hail("table", TABLES)
    place(target_ref, offset_ref, slot_ref, source_ref, request_ref, rank_ref)
    gather_in(TABLES)

    def ask(d, carry):
        peer = lax.rem(me + d, TABLES)
        push("table", peer, request_ref.at[peer], wanted_ref.at[me], sent_ask.at[d], got_ask.at[d]).start()
        return carry

    lax.fori_loop(1, TABLES, ask, 0)
    wanted_ref[me] = request_ref[me]
    finish(me, request_ref, wanted_ref, sent_ask, got_ask)
    clip_ref[...] = jnp.clip(wanted_ref[...], 0, ROWS - 1)
    copy = pltpu.make_async_copy(clip_ref, index_ref, copied)
    copy.start()
    copy.wait()
    trade(me, index_ref, table_ref, block_ref, rows_ref, back_ref, sent, got)


def fetch(target, offset, table):
    lists = (TABLES, CAP // LANES, LANES)
    return pl.pallas_call(
        fetch_kernel,
        out_shape=(
            jax.ShapeDtypeStruct((FEATS, BATCH), i32),
            jax.ShapeDtypeStruct(lists, i32),
            jax.ShapeDtypeStruct(lists, i32),
            jax.ShapeDtypeStruct((TABLES, CAP, WIDTH), bf16),
        ),
        in_specs=[vmem()] * 3,
        out_specs=(vmem(),) * 4,
        scratch_shapes=[
            pltpu.VMEM((FEATS, BATCH), i32),
            pltpu.VMEM(lists, i32),
            pltpu.VMEM(lists, i32),
            pltpu.SMEM(lists, i32),
            pltpu.VMEM((CAP, WIDTH), f32),
            pltpu.VMEM((TABLES, CAP, WIDTH), bf16),
            pltpu.SemaphoreType.DMA,
            dma(TABLES),
            dma(TABLES),
            dma(TABLES),
            dma(TABLES),
        ],
        compiler_params=params(2),
        name="fetch",
    )(target, offset, table)


def mix_kernel(
    slot_ref, back_ref, weight_ref, label_ref, last_ref, pooled_ref, slope_ref,
    table_ref, block_ref, sum_ref, arrived_ref, sent, got, sent_slope, got_slope,
):
    me = lax.axis_index("group")
    hail("group", GROUPS)

    def widen(t, carry):
        table_ref[pl.ds(pl.multiple_of(t * CAP, CAP), CAP), :] = back_ref[t].astype(f32)
        return carry

    lax.fori_loop(0, TABLES, widen, 0)
    gather_in(GROUPS)

    def part(ref, index):
        return ref.at[pl.ds(pl.multiple_of(index * SHARE, SHARE), SHARE)]

    def pair(k, carry):
        first = lax.rem(me // 2 + 1 + k, GROUPS // 2) * 2
        base = pl.multiple_of(first * SHARE, 2 * SHARE)

        def group(b, inner):
            at = pl.multiple_of(b * 8, 8)
            for j in range(8):
                for f in range(FEATS):
                    row = slot_ref[f * BATCH + base + at + j]
                    block_ref[f, pl.ds(at + j, 1), :] = table_ref[pl.ds(row, 1), :]
            return inner

        lax.fori_loop(0, 2 * SHARE // 8, group, 0)
        pooled = jnp.concatenate([block_ref[f].astype(bf16) for f in range(FEATS)], axis=1)
        both = pl.ds(base, 2 * SHARE)
        pooled_ref[both, :] = pooled
        sum_ref[both, :] = jnp.dot(pooled, weight_ref[...], preferred_element_type=f32)
        for e in range(2):
            peer = first + e
            d = lax.rem(peer + GROUPS - me, GROUPS)

            @pl.when(d > 0)
            def _():
                push("group", peer, part(sum_ref, peer), arrived_ref.at[d], sent.at[d], got.at[d]).start()

        return carry

    lax.fori_loop(0, GROUPS // 2, pair, 0)
    mine = pl.ds(pl.multiple_of(me * SHARE, SHARE), SHARE)
    pre_act = sum_ref[mine, :]
    for d in range(1, GROUPS):
        peer = lax.rem(me + d, GROUPS)
        push("group", peer, part(sum_ref, peer), arrived_ref.at[d], sent.at[d], got.at[d]).wait()
        pre_act = pre_act + arrived_ref[d]
    sig_pre = jax.nn.sigmoid(pre_act)
    last = last_ref[...]
    logits = jnp.sum(pre_act * sig_pre * last, axis=1, keepdims=True)
    residual = jax.nn.sigmoid(logits) - label_ref[...]
    slope_ref[mine, :] = (residual * last * (sig_pre * (1.0 + pre_act * (1.0 - sig_pre)))).astype(bf16)
    for d in range(1, GROUPS):
        peer = lax.rem(me + d, GROUPS)
        push("group", peer, part(slope_ref, me), part(slope_ref, me), sent_slope.at[d], got_slope.at[d]).start()
    for d in range(1, GROUPS):
        peer = lax.rem(me + d, GROUPS)
        giver = lax.rem(me + GROUPS - d, GROUPS)
        push("group", peer, part(slope_ref, me), part(slope_ref, giver), sent_slope.at[d], got_slope.at[d]).wait()


def mix(slot, back, weight, label, last):
    return pl.pallas_call(
        mix_kernel,
        out_shape=(
            jax.ShapeDtypeStruct((BATCH, FEATS * WIDTH), bf16),
            jax.ShapeDtypeStruct((BATCH, HIDDEN), bf16),
        ),
        in_specs=[smem()] + [vmem()] * 4,
        out_specs=(vmem(), vmem()),
        scratch_shapes=[
            pltpu.VMEM((TABLES * CAP, WIDTH), f32),
            pltpu.VMEM((FEATS, 2 * SHARE, WIDTH), f32),
            pltpu.VMEM((BATCH, HIDDEN), f32),
            pltpu.VMEM((GROUPS, SHARE, HIDDEN), f32),
            dma(GROUPS),
            dma(GROUPS),
            dma(GROUPS),
            dma(GROUPS),
        ],
        compiler_params=params(0),
        name="mix",
    )(slot, back, weight, label, last)


def give_kernel(source_ref, slope_ref, weight_ref, back_ref, table_ref, block_ref, rows_ref, sent, got):
    me = lax.axis_index("table")
    hail("table", TABLES)

    def pair(k, carry):
        at = pl.multiple_of(k * 2 * WIDTH, 2 * WIDTH)
        both = dot_nt(slope_ref[...], weight_ref[pl.ds(at, 2 * WIDTH), :]).astype(bf16).astype(f32)
        to = pl.multiple_of(k * 2 * BATCH, 2 * BATCH)
        table_ref[pl.ds(to, BATCH), :] = both[:, :WIDTH]
        table_ref[pl.ds(to + BATCH, BATCH), :] = both[:, WIDTH:]
        return carry

    lax.fori_loop(0, FEATS // 2, pair, 0)
    gather_in(TABLES)
    trade(me, source_ref, table_ref, block_ref, rows_ref, back_ref, sent, got)


def give(source, slope, weight):
    return pl.pallas_call(
        give_kernel,
        out_shape=jax.ShapeDtypeStruct((TABLES, CAP, WIDTH), bf16),
        in_specs=[smem(), vmem(), vmem()],
        out_specs=vmem(),
        scratch_shapes=[
            pltpu.VMEM((FEATS * BATCH, WIDTH), f32),
            pltpu.VMEM((CAP, WIDTH), f32),
            pltpu.VMEM((TABLES, CAP, WIDTH), bf16),
            dma(TABLES),
            dma(TABLES),
        ],
        compiler_params=params(3),
        name="give",
    )(source, slope, weight)


def update_kernel(
    index_ref, count_ref, slot_ref, incoming_ref, table_ref, state_ref, rows_ref, new_state_ref, stripes_ref, block_ref, *accs
):
    def clear(k, carry):
        at = pl.ds(pl.multiple_of(k * 128, 128), 128)
        for acc in accs:
            acc[at, :] = jnp.zeros((128, WIDTH), f32)
        return carry

    lax.fori_loop(0, ROWS // 128, clear, 0)

    def peer(t, carry):
        block_ref[...] = incoming_ref[t].astype(f32)

        def group(k, inner):
            at = pl.multiple_of(k * ACCS, ACCS)
            for j in range(ACCS):
                row = index_ref[t * CAP + at + j]
                accs[j][pl.ds(row, 1), :] = accs[j][pl.ds(row, 1), :] + block_ref[pl.ds(at + j, 1), :]
            return inner

        return lax.fori_loop(0, (count_ref[t] + ACCS - 1) // ACCS, group, carry)

    lax.fori_loop(0, TABLES, peer, 0)
    half = WIDTH // 2
    same = iota((WIDTH, WIDTH), 0) == iota((WIDTH, WIDTH), 1)

    def stripe(s, carry):
        at = pl.ds(pl.multiple_of(s * 128, 128), 128)
        grad = accs[0][at, :]
        for acc in accs[1:]:
            grad = grad + acc[at, :]
        mean = jnp.sum(grad * grad, axis=1, keepdims=True) * (1.0 / WIDTH)
        state = jnp.sum(jnp.where(same, state_ref[pl.ds(s, 1), :], 0.0), axis=1, keepdims=True) + mean
        change = -LEARN_RATE * grad * lax.rsqrt(state)
        rows_ref[at, :] = table_ref[at, :] + change
        new_state_ref[pl.ds(s, 1), :] = jnp.sum(jnp.where(same, state, 0.0), axis=0, keepdims=True)
        stripes_ref[slot_ref[s]] = (change[:half] + change[half:]).astype(bf16)
        return carry

    lax.fori_loop(0, ROWS // 128, stripe, 0)


def update(index, count, slot, incoming, table, state):
    return pl.pallas_call(
        update_kernel,
        out_shape=(
            jax.ShapeDtypeStruct((ROWS, WIDTH), f32),
            jax.ShapeDtypeStruct((ROWS // WIDTH, WIDTH), f32),
            jax.ShapeDtypeStruct((ROWS // WIDTH, WIDTH // 2, WIDTH), bf16),
        ),
        in_specs=[smem(), smem(), smem(), vmem(), vmem(), vmem()],
        out_specs=(vmem(),) * 3,
        scratch_shapes=[pltpu.VMEM((CAP, WIDTH), f32)] + [pltpu.VMEM((ROWS + 8, WIDTH), f32)] * ACCS,
        compiler_params=params(),
        name="update",
    )(index, count, slot, incoming, table, state)


def stripe_kernel(stripes_ref, parity_ref, out_ref, arrived_ref, sent, got):
    me = lax.axis_index("group")
    hail("group", GROUPS)
    gather_in(GROUPS)
    copies = []
    for d in range(1, GROUPS):
        peer = lax.rem(me + d, GROUPS)
        theirs = stripes_ref.at[pl.ds(peer * OWNED, OWNED)]
        copies.append(push("group", peer, theirs, arrived_ref.at[d], sent.at[d], got.at[d]))
        copies[-1].start()
    total = stripes_ref[pl.ds(me * OWNED, OWNED)].astype(f32)
    for copy in copies:
        copy.wait_recv()
    for d in range(1, GROUPS):
        total = total + arrived_ref[d].astype(f32)
    out_ref[...] = parity_ref[...] + total
    for copy in copies:
        copy.wait_send()


def stripe_sum(stripes, parity):
    return pl.pallas_call(
        stripe_kernel,
        out_shape=jax.ShapeDtypeStruct(parity.shape, f32),
        in_specs=[vmem()] * 2,
        out_specs=vmem(),
        scratch_shapes=[pltpu.VMEM((GROUPS,) + parity.shape, bf16)] + [pltpu.SemaphoreType.DMA((GROUPS,))] * 2,
        compiler_params=params(1),
        name="stripe_sum",
    )(stripes, parity)


def local(
    table_rows,
    row_state,
    parity,
    parity_slot,
    row_shard,
    row_offset,
    labels,
    first_weight,
    last_weight,
):
    table = table_rows[0]
    target = jnp.transpose(row_shard[0, :, :, 0])
    offset = jnp.transpose(row_offset[0])
    slot, source, wanted, back = fetch(target, offset, table)
    own = lax.dynamic_slice(labels, (lax.axis_index("group") * SHARE,), (SHARE,)).astype(f32)
    pooled, slope = mix(slot.reshape(-1), back, first_weight, own[:, None], last_weight[None, :])
    weight_grad = lax.dot_general(slope, pooled, (((0,), (0,)), ((), ())), preferred_element_type=f32)
    slope, weight_grad = lax.optimization_barrier((slope, weight_grad))
    first_grad = lax.psum_scatter(weight_grad, "table", scatter_dimension=0, tiled=True)
    incoming = give(source, slope, first_weight)
    served = jnp.sum((wanted >= 0).astype(i32), axis=(1, 2))
    segment = jnp.where(wanted >= 0, wanted, ROWS).reshape(-1)
    new_rows, new_state, stripes = update(
        segment, served, parity_slot[0], incoming, table, row_state.reshape(ROWS // WIDTH, WIDTH)
    )
    new_parity = stripe_sum(stripes, parity[0])
    return (new_rows[None], new_state.reshape(1, ROWS), new_parity[None], first_grad)


def solution(mesh):
    placed = (
        P("group", "table", None),
        P("group", "table"),
        P("table", "group", None, None),
        P("table", None),
        P("group", "table", None, None),
        P("group", "table", None),
        P("table"),
        P("group", None),
        P(),
    )
    return jax.shard_map(
        local,
        mesh=mesh,
        in_specs=placed,
        out_specs=(
            P("group", "table", None),
            P("group", "table"),
            P("table", "group", None, None),
            P("table", "group"),
        ),
        check_vma=False,
    )
```

time: 681 us -> 417 us (0.61)
  waiting for transfers between devices: 436 us -> 20.9 us
  Pallas kernels: 76.4 us -> 366 us
  blocking collectives: 122 us -> 0 us
  starting transfers between devices: 13.4 us -> 0.04 us
    pallas_call x4, Pallas kernels: 56.6 us -> 346 us  [the longest x1 137 us: fetch(): pl.pallas_call(fetch_kernel, out_shape=(jax.ShapeDtypeStruct((FEATS, BATC...]
    reduce_scatter x2 -> x0, waiting for transfers between devices: 158 us -> none  [the longest x1 82.9 us: local(): lax.psum_scatter(stripes, 'group', scatter_dimension=0, tiled=True)]
    all_to_all x2 -> x0, blocking collectives: 122 us -> none  [the longest x1 104 us: local(): lax.all_to_all(outgoing, 'table', split_axis=0, concat_axis=0, tiled=True)]
    reduce_scatter x1, waiting for transfers between devices: 133 us -> 20.9 us  [local(): lax.psum_scatter(weight_grad, 'table', scatter_dimension=0, tiled=True)]
    all_to_all x1 -> x0, waiting for transfers between devices: 96 us -> none  [local(): lax.all_to_all(rows_out, 'table', split_axis=0, concat_axis=0, tiled=True)]
    all_gather x1 -> x0, waiting for transfers between devices: 49.1 us -> none  [local(): lax.all_gather(head_slope(share, own, last_weight), 'group', axis=0, tile...]
    all_to_all x1 -> x0, starting transfers between devices: 13.2 us -> none  [local(): lax.all_to_all(rows_out, 'table', split_axis=0, concat_axis=0, tiled=True)]
  transfers between devices with their start and end apart: 5 -> 1, of which waited for: 5 -> 1; matrix products, arithmetic and copies ran while one was open for 1% -> 0% of each run, Pallas kernels for 0% -> 42%
where the time goes in v3:
time: 417 us; the launch traced here: 416 us
  Pallas kernels  366 us (88%)
  waiting for transfers between devices  20.9 us (5%)
  between operations  14.1 us (3%)
  matrix products  7.53 us (2%)
  local copies, waits for them, and re-layouts  5.04 us (1%)
    pallas_call x1, Pallas kernels, fetch(): pl.pallas_call(fetch_kernel, out_shape=(jax.ShapeDtypeStruct((FEATS, BATC...  137 us
    pallas_call x1, Pallas kernels, give(): pl.pallas_call(give_kernel, out_shape=jax.ShapeDtypeStruct((TABLES, CAP,...  134 us
    pallas_call x1, Pallas kernels, mix(): pl.pallas_call(mix_kernel, out_shape=(jax.ShapeDtypeStruct((BATCH, FEATS...  54.1 us
    reduce_scatter x1, waiting for transfers between devices, local(): lax.psum_scatter(weight_grad, 'table', scatter_dimension=0, tiled=True)  20.9 us
    pallas_call x1, Pallas kernels, stripe_sum(): pl.pallas_call(stripe_kernel, out_shape=jax.ShapeDtypeStruct(parity.shape...  20.7 us
    pallas_call x1, Pallas kernels, update(): pl.pallas_call(update_kernel, out_shape=(jax.ShapeDtypeStruct((ROWS, WIDT...  20.5 us
  transfers between devices with their start and end apart: 1, of which 1 were waited for; matrix products, arithmetic and copies ran while one was open for 0% of the time, Pallas kernels for 42%

profile of v3, /device:TPU:16, one launch (start us, length us, event | category | flops | bytes accessed | tf_op | source)
XLA Modules:
  0.0 416.4 jit_solution(14162248783017515796)
XLA Ops:
  7.2 0.0 reduce-scatter.2.cloned.1.call-start
  7.2 0.8 convert_bitcast_fusion
  8.0 0.7 copy.13.label_ref
  8.7 1.4 copy.17
  10.1 136.6 %fetch.1 = (s32[16,512]{1,0:T(8,128)}, s32[32,4,128]{2,1,0:T(4,128)}, s32[32,4,128]{2,1,0:T(4,128)}, bf16[32,512,128]{2,1,0:T(8,128)(2,1)}) custom-call(s32[16,512]{1,0:T(8,128)} %bitcast.28, s32[16,512]{1,0:T(8,128)} %bitcast.30, f32[4096,128]{1,0:T(8,128)} %bitcast.23), custom_call_target="tpu_custom_call" | custom-call | tf_op jit(solution)/shard_map/fetch/pallas_call | solution.py:181
  146.7 1.4 copy.15
  148.1 54.1 %mix.1 = (bf16[512,2048]{1,0:T(8,128)(2,1)}, bf16[512,1024]{1,0:T(8,128)(2,1)}) custom-call(s32[8192]{0:T(1024)} %bitcast.27, bf16[32,512,128]{2,1,0:T(8,128)(2,1)} %get-tuple-element.18.back_ref, bf16[2048,1024]{1,0:T(8,128)(2,1)} %weight_ref.3, f32[64,1]{1,0:T(8,128)} %copy.13.label_ref, f32[1,1024]{1,0:T(1,128)} %bitcast.33), custom_call_target="tpu_custom_call" | custom-call | tf_op jit(solution)/shard_map/mix/pallas_call | solution.py:275
  202.2 7.5 %fusion.1 = f32[1024,2048]{1,0:T(8,128)} fusion(bf16[512,1024]{1,0:T(8,128)(2,1)} %get-tuple-element.21.slope_ref, bf16[512,2048]{1,0:T(8,128)(2,1)} %get-tuple-element.20), kind=kOutput, calls=%fused_computation.5 | convolution fusion | flops 2147483648 | bytes 11534336 | tf_op jit(solution)/shard_map/dot_general | solution.py:441
  209.7 0.0 reduce-scatter.2.cloned.1.call-update
  209.8 0.0 copy-start
  209.8 134.3 %give.1.incoming_ref = bf16[32,512,128]{2,1,0:T(8,128)(2,1)} custom-call(s32[32,4,128]{2,1,0:T(4,128)} %get-tuple-element.16.source_ref, bf16[512,1024]{1,0:T(8,128)(2,1)} %get-tuple-element.21.slope_ref, bf16[2048,1024]{1,0:T(8,128)(2,1)} %weight_ref.3), custom_call_target="tpu_custom_call" | custom-call | tf_op jit(solution)/shard_map/give/pallas_call | solution.py:316
  344.1 0.0 copy-done
  344.1 1.8 fusion
  345.9 20.5 %update.1 = (f32[4096,128]{1,0:T(8,128)}, f32[32,128]{1,0:T(8,128)}, bf16[32,64,128]{2,1,0:T(8,128)(2,1)}) custom-call(s32[16384]{0:T(1024)} %bitcast.26, s32[32]{0:T(128)} %get-tuple-element.26.count_ref, s32[32]{0:T(128)} %bitcast.34, bf16[32,512,128]{2,1,0:T(8,128)(2,1)} %give.1.incoming_ref, f32[4096,128]{1,0:T(8,128)} %bitcast.24, f32[32,128]{1,0:T(8,128)} %bitcast.32), custom_call_target="tpu_custom_call" | custom-call | tf_op jit(solution)/shard_map/update/pallas_call | solution.py:377
  366.4 20.7 %stripe_sum.1 = f32[4,64,128]{2,1,0:T(8,128)} custom-call(bf16[32,64,128]{2,1,0:T(8,128)(2,1)} %get-tuple-element.24.stripes_ref, f32[4,64,128]{2,1,0:T(8,128)} %bitcast.29), custom_call_target="tpu_custom_call" | custom-call | tf_op jit(solution)/shard_map/stripe_sum/pallas_call | solution.py:413
  387.1 20.9 %reduce-scatter.2.cloned.1.call-done = f32[32,2048]{1,0:T(8,128)} async-done(((f32[1024,2048]{1,0:T(8,128)}), f32[32,2048]{1,0:T(8,128)}) %reduce-scatter.2.cloned.1.call-update) | async-done | bytes 262160 | tf_op jit(solution)/shard_map/reduce_scatter | solution.py:443
  408.0 1.6 copy.19
Async XLA Ops:
  7.2 400.8 %reduce-scatter.2.cloned.1.call-start = ((), (), s32[]{:S(2)}) async-start(), calls=%async_computation.1 | async-start | bytes 8650752 | tf_op jit(solution)/shard_map/reduce_scatter | solution.py:443
  209.8 134.3 %copy-start = (s32[32,4,128]{2,1,0:T(4,128)S(1)}, s32[32,4,128]{2,1,0:T(4,128)}, u32[]{:S(2)}) copy-start(s32[32,4,128]{2,1,0:T(4,128)} %get-tuple-element.15) | copy-start | bytes 196612
Sparse Core Ops, SparseCore 0:
  209.9 198.0 reduce-scatter.1

commit v4 on v3

--- a/solution.py
+++ b/solution.py
@@ -17,6 +17,10 @@
 PER_FEATURE = 256
 WIDTH = 128
 HIDDEN = 1024
+NEAR = 4
+PLANES = TABLES // NEAR
+OUT_ROWS = HIDDEN // TABLES
+EARLY = 9
 SHARE = BATCH // GROUPS
 OWNED = 32 // GROUPS
 LANES = 128
@@ -128,24 +132,32 @@
         lax.fori_loop(0, LANES // GROUP_OF, group, 0)
 
 
-def trade(me, index_ref, table_ref, block_ref, rows_ref, back_ref, sent, got):
+def trade(me, first, last, index_ref, table_ref, block_ref, rows_ref, back_ref, sent, got):
     def serve(d, carry):
-        peer = lax.rem(me + d, TABLES)
+        peer, _ = route(me, d)
         pick(index_ref, peer, table_ref, block_ref)
         rows_ref[peer] = block_ref[...].astype(bf16)
         push("table", peer, rows_ref.at[peer], back_ref.at[me], sent.at[d], got.at[d]).start()
         return carry
 
-    lax.fori_loop(1, TABLES, serve, 0)
-    pick(index_ref, me, table_ref, block_ref)
-    back_ref[me] = block_ref[...].astype(bf16)
-    finish(me, rows_ref, back_ref, sent, got)
+    lax.fori_loop(first, last, serve, 0)
+    if last == TABLES:
+        pick(index_ref, me, table_ref, block_ref)
+        back_ref[me] = block_ref[...].astype(bf16)
+
+
+def route(me, k):
+    z, q = me // NEAR, lax.rem(me, NEAR)
+    turn, step = lax.rem(k, PLANES), k // PLANES
+    by = (turn + 1) // 2 * (2 * lax.rem(turn, 2) - 1)
+    peer = lax.rem(z + by + PLANES, PLANES) * NEAR + lax.rem(q + step, NEAR)
+    giver = lax.rem(z - by + PLANES, PLANES) * NEAR + lax.rem(q - step + NEAR, NEAR)
+    return peer, giver
 
 
 def finish(me, rows_ref, back_ref, sent, got):
     def settle(d, carry):
-        peer = lax.rem(me + d, TABLES)
-        giver = lax.rem(me + TABLES - d, TABLES)
+        peer, giver = route(me, d)
         push("table", peer, rows_ref.at[peer], back_ref.at[giver], sent.at[d], got.at[d]).wait()
         return carry
 
@@ -162,7 +174,7 @@
     gather_in(TABLES)
 
     def ask(d, carry):
-        peer = lax.rem(me + d, TABLES)
+        peer, _ = route(me, d)
         push("table", peer, request_ref.at[peer], wanted_ref.at[me], sent_ask.at[d], got_ask.at[d]).start()
         return carry
 
@@ -173,7 +185,8 @@
     copy = pltpu.make_async_copy(clip_ref, index_ref, copied)
     copy.start()
     copy.wait()
-    trade(me, index_ref, table_ref, block_ref, rows_ref, back_ref, sent, got)
+    trade(me, 1, TABLES, index_ref, table_ref, block_ref, rows_ref, back_ref, sent, got)
+    finish(me, rows_ref, back_ref, sent, got)
 
 
 def fetch(target, offset, table):
@@ -295,8 +308,13 @@
     )(slot, back, weight, label, last)
 
 
-def give_kernel(source_ref, slope_ref, weight_ref, back_ref, table_ref, block_ref, rows_ref, sent, got):
+def give_kernel(
+    source_ref, slope_ref, pooled_ref, weight_ref, back_ref, packed_ref,
+    table_ref, block_ref, rows_ref, grad_ref, near_ref, across_ref, sent, got, sent_near, got_near, sent_across, got_across,
+):
     me = lax.axis_index("table")
+    core, side = lax.rem(me, 2), lax.rem(me // 2, 2)
+    other, across = me + 1 - 2 * core, me + 2 - 4 * side
     hail("table", TABLES)
 
     def pair(k, carry):
@@ -309,25 +327,90 @@
 
     lax.fori_loop(0, FEATS // 2, pair, 0)
     gather_in(TABLES)
-    trade(me, source_ref, table_ref, block_ref, rows_ref, back_ref, sent, got)
-
-
-def give(source, slope, weight):
+    trade(me, 1, EARLY, source_ref, table_ref, block_ref, rows_ref, back_ref, sent, got)
+
+    def to_near(z):
+        return push("table", other, grad_ref.at[z, :, 1 - core], near_ref.at[z], sent_near.at[z], got_near.at[z])
+
+    def to_across(z):
+        return push("table", across, grad_ref.at[z, 1 - side, core], across_ref.at[z], sent_across.at[z], got_across.at[z])
+
+    def outer(z, carry):
+        at = pl.multiple_of(z * LANES, LANES)
+        part = lax.dot_general(
+            slope_ref[:, pl.ds(at, LANES)], pooled_ref[...], (((0,), (0,)), ((), ())), preferred_element_type=f32
+        )
+        grad_ref[z] = part.reshape(grad_ref.shape[1:])
+        to_near(z).start()
+        return carry
+
+    lax.fori_loop(0, PLANES, outer, 0)
+    trade(me, EARLY, TABLES, source_ref, table_ref, block_ref, rows_ref, back_ref, sent, got)
+
+    def fold(z, carry):
+        to_near(z).wait()
+        for x in range(2):
+            grad_ref[z, x, core] = grad_ref[z, x, core] + near_ref[z, x]
+        to_across(z).start()
+        return carry
+
+    lax.fori_loop(0, PLANES, fold, 0)
+
+    def seal(z, carry):
+        to_across(z).wait()
+        total = grad_ref[z, side, core] + across_ref[z]
+        top = jnp.max(jnp.abs(total), axis=1, keepdims=True)
+        power = jnp.ceil(jnp.log2(jnp.clip(top * 1.0001, 1e-30, 1e30))) - 15.0
+        scaled = jnp.floor(total * jnp.exp2(-power) + 0.5).astype(i32)
+        k = lax.rem(z - me // NEAR + PLANES, PLANES)
+        packed_ref[k, :, : FEATS * WIDTH] = scaled.astype(jnp.int16)
+        packed_ref[k, :, FEATS * WIDTH :] = jnp.broadcast_to(power.astype(i32), (OUT_ROWS, LANES)).astype(jnp.int16)
+        return carry
+
+    lax.fori_loop(0, PLANES, seal, 0)
+    finish(me, rows_ref, back_ref, sent, got)
+
+
+def give(source, slope, pooled, weight):
+    piece = (OUT_ROWS, FEATS * WIDTH)
     return pl.pallas_call(
         give_kernel,
-        out_shape=jax.ShapeDtypeStruct((TABLES, CAP, WIDTH), bf16),
-        in_specs=[smem(), vmem(), vmem()],
-        out_specs=vmem(),
+        out_shape=(
+            jax.ShapeDtypeStruct((TABLES, CAP, WIDTH), bf16),
+            jax.ShapeDtypeStruct((PLANES, OUT_ROWS, FEATS * WIDTH + LANES), jnp.int16),
+        ),
+        in_specs=[smem(), vmem(), vmem(), vmem()],
+        out_specs=(vmem(), vmem()),
         scratch_shapes=[
             pltpu.VMEM((FEATS * BATCH, WIDTH), f32),
             pltpu.VMEM((CAP, WIDTH), f32),
             pltpu.VMEM((TABLES, CAP, WIDTH), bf16),
+            pltpu.VMEM((PLANES, 2, 2) + piece, f32),
+            pltpu.VMEM((PLANES, 2) + piece, f32),
+            pltpu.VMEM((PLANES,) + piece, f32),
             dma(TABLES),
             dma(TABLES),
+            dma(PLANES),
+            dma(PLANES),
+            dma(PLANES),
+            dma(PLANES),
         ],
         compiler_params=params(3),
         name="give",
-    )(source, slope, weight)
+    )(source, slope, pooled, weight)
+
+
+def unpack(packed):
+    power = packed[:, FEATS * WIDTH : FEATS * WIDTH + 1].astype(f32)
+    return packed[:, : FEATS * WIDTH].astype(f32) * jnp.exp2(power)
+
+
+def sum_planes(packed):
+    total = unpack(packed[0])
+    for k in range(1, PLANES):
+        ring = [(t, (t + NEAR * k) % TABLES) for t in range(TABLES)]
+        total = total + unpack(lax.ppermute(packed[k], "table", ring))
+    return total
 
 
 def update_kernel(
@@ -438,10 +521,8 @@
     slot, source, wanted, back = fetch(target, offset, table)
     own = lax.dynamic_slice(labels, (lax.axis_index("group") * SHARE,), (SHARE,)).astype(f32)
     pooled, slope = mix(slot.reshape(-1), back, first_weight, own[:, None], last_weight[None, :])
-    weight_grad = lax.dot_general(slope, pooled, (((0,), (0,)), ((), ())), preferred_element_type=f32)
-    slope, weight_grad = lax.optimization_barrier((slope, weight_grad))
-    first_grad = lax.psum_scatter(weight_grad, "table", scatter_dimension=0, tiled=True)
-    incoming = give(source, slope, first_weight)
+    incoming, packed = give(source, slope, pooled, first_weight)
+    first_grad = sum_planes(packed)
     served = jnp.sum((wanted >= 0).astype(i32), axis=(1, 2))
     segment = jnp.where(wanted >= 0, wanted, ROWS).reshape(-1)
     new_rows, new_state, stripes = update(

time: 417 us -> 385 us (0.923)
  Pallas kernels: 366 us -> 345 us
  starting transfers between devices: 0.04 us -> 20.1 us
  waiting for transfers between devices: 20.9 us -> 5.63 us
  between operations: 14.1 us -> 0.74 us
  matrix products: 7.53 us -> 0 us
    reduce_scatter x1 -> x0, waiting for transfers between devices: 20.9 us -> none  [local(): lax.psum_scatter(weight_grad, 'table', scatter_dimension=0, tiled=True)]
    ppermute x0 -> x7, starting transfers between devices: none -> 20.1 us  [sum_planes(): total = total + unpack(lax.ppermute(packed[k], 'table', ring))]
    pallas_call x1, Pallas kernels: 137 us -> 119 us  [fetch(): pl.pallas_call(fetch_kernel, out_shape=(jax.ShapeDtypeStruct((FEATS, BATC...]
    pallas_call x1, Pallas kernels: 20.7 us -> 12.5 us  [stripe_sum(): pl.pallas_call(stripe_kernel, out_shape=jax.ShapeDtypeStruct(parity.shape...]
    dot_general x1 -> x0, matrix products: 7.53 us -> none  [local(): lax.dot_general(slope, pooled, (((0,), (0,)), ((), ())), preferred_elemen...]
    ppermute x0 -> x7, waiting for transfers between devices: none -> 5.63 us  [sum_planes(): total = total + unpack(lax.ppermute(packed[k], 'table', ring))]
    pallas_call x1, Pallas kernels: 134 us -> 140 us  [give(): pl.pallas_call(give_kernel, out_shape=(jax.ShapeDtypeStruct((TABLES, CAP,...]
  transfers between devices with their start and end apart: 1 -> 7, of which waited for: 1 -> 2; matrix products, arithmetic and copies ran while one was open for 0% -> 1% of each run, Pallas kernels for 42% -> 8%
where the time goes in v4:
time: 385 us; the launch traced here: 382 us
  Pallas kernels  345 us (90%)
  starting transfers between devices  20.1 us (5%)
  local copies, waits for them, and re-layouts  6.45 us (2%)
  waiting for transfers between devices  5.63 us (1%)
  other arithmetic  4.56 us (1%)
    pallas_call x1, Pallas kernels, give(): pl.pallas_call(give_kernel, out_shape=(jax.ShapeDtypeStruct((TABLES, CAP,...  140 us
    pallas_call x1, Pallas kernels, fetch(): pl.pallas_call(fetch_kernel, out_shape=(jax.ShapeDtypeStruct((FEATS, BATC...  119 us
    pallas_call x1, Pallas kernels, mix(): pl.pallas_call(mix_kernel, out_shape=(jax.ShapeDtypeStruct((BATCH, FEATS...  53.9 us
    ppermute x7, starting transfers between devices, sum_planes(): total = total + unpack(lax.ppermute(packed[k], 'table', ring))  20.1 us
    pallas_call x1, Pallas kernels, update(): pl.pallas_call(update_kernel, out_shape=(jax.ShapeDtypeStruct((ROWS, WIDT...  19.5 us
    pallas_call x1, Pallas kernels, stripe_sum(): pl.pallas_call(stripe_kernel, out_shape=jax.ShapeDtypeStruct(parity.shape...  12.5 us
  transfers between devices with their start and end apart: 7, of which 2 were waited for; matrix products, arithmetic and copies ran while one was open for 1% of the time, Pallas kernels for 8%

profile of v4, /device:TPU:16, one launch (start us, length us, event | category | flops | bytes accessed | tf_op | source)
XLA Modules:
  0.0 382.3 jit_solution(13653277191303432718)
XLA Ops:
  0.6 0.8 convert_bitcast_fusion
  1.4 0.7 copy.14.label_ref
  2.1 1.4 copy.18
  3.5 119.2 %fetch.1 = (s32[16,512]{1,0:T(8,128)}, s32[32,4,128]{2,1,0:T(4,128)}, s32[32,4,128]{2,1,0:T(4,128)}, bf16[32,512,128]{2,1,0:T(8,128)(2,1)}) custom-call(s32[16,512]{1,0:T(8,128)} %bitcast.42, s32[16,512]{1,0:T(8,128)} %bitcast.44, f32[4096,128]{1,0:T(8,128)} %bitcast.37), custom_call_target="tpu_custom_call" | custom-call | tf_op jit(solution)/shard_map/fetch/pallas_call | solution.py:194
  122.7 1.4 copy.16
  124.1 53.9 %mix.1 = (bf16[512,2048]{1,0:T(8,128)(2,1)}, bf16[512,1024]{1,0:T(8,128)(2,1)}) custom-call(s32[8192]{0:T(1024)} %bitcast.41, bf16[32,512,128]{2,1,0:T(8,128)(2,1)} %get-tuple-element.18.back_ref, bf16[2048,1024]{1,0:T(8,128)(2,1)} %weight_ref.3, f32[64,1]{1,0:T(8,128)} %copy.14.label_ref, f32[1,1024]{1,0:T(1,128)} %bitcast.47), custom_call_target="tpu_custom_call" | custom-call | tf_op jit(solution)/shard_map/mix/pallas_call | solution.py:288
  178.0 139.6 %give.1 = (bf16[32,512,128]{2,1,0:T(8,128)(2,1)}, s16[8,32,2176]{2,1,0:T(8,128)(2,1)}) custom-call(s32[32,4,128]{2,1,0:T(4,128)} %get-tuple-element.16.source_ref, bf16[512,1024]{1,0:T(8,128)(2,1)} %get-tuple-element.19.slope_ref, bf16[512,2048]{1,0:T(8,128)(2,1)} %get-tuple-element.20.pooled_ref, bf16[2048,1024]{1,0:T(8,128)(2,1)} %weight_ref.3), custom_call_target="tpu_custom_call" | custom-call | tf_op jit(solution)/shard_map/give/pallas_call | solution.py:376
  317.6 0.0 copy-start
  317.6 1.4 slice_bitcast_fusion.7
  319.0 0.4 collective-permute-start.6
  319.5 0.8 collective-permute-start.5
  320.3 3.7 collective-permute-start.4
  324.0 2.3 collective-permute-start.3
  326.3 3.3 collective-permute-start.2
  329.6 0.0 copy-done
  329.6 1.7 fusion
  331.3 0.1 exponential_reduce_fusion.7
  331.5 19.5 %update.1 = (f32[4096,128]{1,0:T(8,128)}, f32[32,128]{1,0:T(8,128)}, bf16[32,64,128]{2,1,0:T(8,128)(2,1)}) custom-call(s32[16384]{0:T(1024)} %bitcast.40, s32[32]{0:T(128)} %get-tuple-element.34.count_ref, s32[32]{0:T(128)} %bitcast.48, bf16[32,512,128]{2,1,0:T(8,128)(2,1)} %get-tuple-element.21.incoming_ref, f32[4096,128]{1,0:T(8,128)} %bitcast.38, ...), custom_call_target="tpu_custom_call" | custom-call | tf_op jit(solution)/shard_map/update/pallas_call | solution.py:460
  351.0 12.5 %stripe_sum.1 = f32[4,64,128]{2,1,0:T(8,128)} custom-call(bf16[32,64,128]{2,1,0:T(8,128)(2,1)} %get-tuple-element.24.stripes_ref, f32[4,64,128]{2,1,0:T(8,128)} %bitcast.43), custom_call_target="tpu_custom_call" | custom-call | tf_op jit(solution)/shard_map/stripe_sum/pallas_call | solution.py:496
  363.5 0.0 collective-permute-done.6
  363.5 9.5 %collective-permute-start.1 = (s16[32,2176]{1,0:T(8,128)(2,1)S(1)}, s16[32,2176]{1,0:T(8,128)(2,1)S(1)}, u32[]{:S(2)}, u32[]{:S(2)}) collective-permute-start(s16[32,2176]{1,0:T(8,128)(2,1)S(1)} %get-tuple-element.32), channel_id=1, source_target_pairs={{0,8},{1,9},{2,10},{3,11},{4,12},{5,13},{6,14},{7,15},{8,16},{9,17... | collective-permute-start | bytes 417800 | tf_op jit(solution)/shard_map/ppermute | solution.py:412
  373.0 0.1 exponential_reduce_fusion
  373.1 0.0 collective-permute-done.5
  373.1 0.1 collective-permute-start
  373.2 0.1 exponential_reduce_fusion.1
  373.3 0.0 collective-permute-done.4
  373.3 0.1 exponential_reduce_fusion.2
  373.4 0.0 collective-permute-done.3
  373.4 0.1 exponential_reduce_fusion.3
  373.6 0.0 collective-permute-done.2
  373.6 0.1 exponential_reduce_fusion.4
  373.7 2.4 collective-permute-done.1
  376.1 0.1 exponential_reduce_fusion.5
  376.3 3.2 collective-permute-done
  379.4 0.1 exponential_reduce_fusion.6
  379.6 1.1 multiply_add_fusion
  380.7 1.6 copy.20
Async XLA Ops:
  317.6 12.0 %copy-start = (s32[32,4,128]{2,1,0:T(4,128)S(1)}, s32[32,4,128]{2,1,0:T(4,128)}, u32[]{:S(2)}) copy-start(s32[32,4,128]{2,1,0:T(4,128)} %get-tuple-element.15) | copy-start | bytes 196612
  319.0 44.5 %collective-permute-start.6 = (s16[32,2176]{1,0:T(8,128)(2,1)S(1)}, s16[32,2176]{1,0:T(8,128)(2,1)S(1)}, u32[]{:S(2)}, u32[]{:S(2)}) collective-permute-start(s16[32,2176]{1,0:T(8,128)(2,1)S(1)} %get-tuple-element.27), channel_id=1, source_target_pairs={{0,28},{1,29},{2,30},{3,31},{4,0},{5,1},{6,2},{7,3},{8,4},{9,5},{1... | collective-permute-start | bytes 417800 | tf_op jit(solution)/shard_map/ppermute | solution.py:412
  319.5 53.6 %collective-permute-start.5 = (s16[32,2176]{1,0:T(8,128)(2,1)S(1)}, s16[32,2176]{1,0:T(8,128)(2,1)S(1)}, u32[]{:S(2)}, u32[]{:S(2)}) collective-permute-start(s16[32,2176]{1,0:T(8,128)(2,1)S(1)} %get-tuple-element.28), channel_id=1, source_target_pairs={{0,24},{1,25},{2,26},{3,27},{4,28},{5,29},{6,30},{7,31},{8,0},{9,1... | collective-permute-start | bytes 417800 | tf_op jit(solution)/shard_map/ppermute | solution.py:412
  320.3 53.0 %collective-permute-start.4 = (s16[32,2176]{1,0:T(8,128)(2,1)S(1)}, s16[32,2176]{1,0:T(8,128)(2,1)S(1)}, u32[]{:S(2)}, u32[]{:S(2)}) collective-permute-start(s16[32,2176]{1,0:T(8,128)(2,1)S(1)} %get-tuple-element.29), channel_id=1, source_target_pairs={{0,20},{1,21},{2,22},{3,23},{4,24},{5,25},{6,26},{7,27},{8,28},{9,... | collective-permute-start | bytes 417800 | tf_op jit(solution)/shard_map/ppermute | solution.py:412
  324.0 49.4 %collective-permute-start.3 = (s16[32,2176]{1,0:T(8,128)(2,1)S(1)}, s16[32,2176]{1,0:T(8,128)(2,1)S(1)}, u32[]{:S(2)}, u32[]{:S(2)}) collective-permute-start(s16[32,2176]{1,0:T(8,128)(2,1)S(1)} %get-tuple-element.30), channel_id=1, source_target_pairs={{0,16},{1,17},{2,18},{3,19},{4,20},{5,21},{6,22},{7,23},{8,24},{9,... | collective-permute-start | bytes 417800 | tf_op jit(solution)/shard_map/ppermute | solution.py:412
  326.3 47.2 %collective-permute-start.2 = (s16[32,2176]{1,0:T(8,128)(2,1)S(1)}, s16[32,2176]{1,0:T(8,128)(2,1)S(1)}, u32[]{:S(2)}, u32[]{:S(2)}) collective-permute-start(s16[32,2176]{1,0:T(8,128)(2,1)S(1)} %get-tuple-element.31), channel_id=1, source_target_pairs={{0,12},{1,13},{2,14},{3,15},{4,16},{5,17},{6,18},{7,19},{8,20},{9,... | collective-permute-start | bytes 417800 | tf_op jit(solution)/shard_map/ppermute | solution.py:412
  363.5 12.6 %collective-permute-start.1 = (s16[32,2176]{1,0:T(8,128)(2,1)S(1)}, s16[32,2176]{1,0:T(8,128)(2,1)S(1)}, u32[]{:S(2)}, u32[]{:S(2)}) collective-permute-start(s16[32,2176]{1,0:T(8,128)(2,1)S(1)} %get-tuple-element.32), channel_id=1, source_target_pairs={{0,8},{1,9},{2,10},{3,11},{4,12},{5,13},{6,14},{7,15},{8,16},{9,17... | collective-permute-start | bytes 417800 | tf_op jit(solution)/shard_map/ppermute | solution.py:412
  373.1 6.3 %collective-permute-start = (s16[32,2176]{1,0:T(8,128)(2,1)S(1)}, s16[32,2176]{1,0:T(8,128)(2,1)S(1)}, u32[]{:S(2)}, u32[]{:S(2)}) collective-permute-start(s16[32,2176]{1,0:T(8,128)(2,1)S(1)} %get-tuple-element.33), channel_id=1, source_target_pairs={{0,4},{1,5},{2,6},{3,7},{4,8},{5,9},{6,10},{7,11},{8,12},{9,13},{1... | collective-permute-start | bytes 417800 | tf_op jit(solution)/shard_map/ppermute | solution.py:412

commit v5 on v4

--- a/solution.py
+++ b/solution.py
@@ -80,7 +80,7 @@
 def place(target_ref, offset_ref, slot_ref, source_ref, request_ref, rank_ref):
     chunks = BATCH // LANES
     lines = chunks * FEATS
-    target = jnp.concatenate([target_ref[:, c * LANES : (c + 1) * LANES] for c in range(chunks)], axis=0)
+    target = target_ref[...]
     row, col = iota((LANES, LANES), 0), iota((LANES, LANES), 1)
     before = (row < col).astype(f32).astype(bf16)
     counter = jnp.concatenate([before, jnp.ones((LANES, LANES), bf16)], axis=1)
@@ -92,20 +92,22 @@
         base = jnp.dot(earlier, counts[:, LANES:].astype(bf16), preferred_element_type=f32)
         rank = rank + named * (counts[:, :LANES] + base)
     rank = rank.astype(i32)
-    rank = jnp.concatenate([rank[c * FEATS : (c + 1) * FEATS] for c in range(chunks)], axis=1)
     rank_ref[...] = rank
-    slot_ref[...] = target_ref[...] * CAP + rank
+    slot_ref[...] = target * CAP + rank
     owner = iota((TABLES, BATCH), 0)
     sample = iota((TABLES, BATCH), 1)
     spot = iota((CAP, BATCH), 0)
 
+    def line(ref, f):
+        return jnp.concatenate([ref[pl.ds(f * chunks + c, 1), :] for c in range(chunks)], axis=1)
+
     def feature(f, total):
-        named = target_ref[pl.ds(f, 1), :] == owner
+        named = line(target_ref, f) == owner
         first = jnp.where(named, f + 1 + 32 * (sample // 256), 0)
         second = jnp.where(named, jnp.broadcast_to(offset_ref[pl.ds(f, 1), :], named.shape), 0)
         third = jnp.where(named, sample % 256, 0)
         values = jnp.concatenate([first, second, third], axis=0).astype(f32).astype(bf16)
-        chosen = (rank_ref[pl.ds(f, 1), :] == spot).astype(f32).astype(bf16)
+        chosen = (line(rank_ref, f) == spot).astype(f32).astype(bf16)
         return total + dot_nt(values, chosen)
 
     total = lax.fori_loop(0, FEATS, feature, jnp.zeros((3 * TABLES, CAP), f32)).astype(i32)
@@ -165,8 +167,8 @@
 
 
 def fetch_kernel(
-    target_ref, offset_ref, table_ref, slot_ref, source_ref, wanted_ref, back_ref,
-    rank_ref, request_ref, clip_ref, index_ref, block_ref, rows_ref, copied, sent_ask, got_ask, sent, got,
+    target_ref, offset_ref, table_ref, slot_ref, source_ref, segment_ref, count_ref, back_ref,
+    rank_ref, request_ref, wanted_ref, clip_ref, index_ref, block_ref, rows_ref, copied, sent_ask, got_ask, sent, got,
 ):
     me = lax.axis_index("table")
     hail("table", TABLES)
@@ -181,9 +183,13 @@
     lax.fori_loop(1, TABLES, ask, 0)
     wanted_ref[me] = request_ref[me]
     finish(me, request_ref, wanted_ref, sent_ask, got_ask)
-    clip_ref[...] = jnp.clip(wanted_ref[...], 0, ROWS - 1)
+    wanted = wanted_ref[...]
+    clip_ref[...] = jnp.clip(wanted, 0, ROWS - 1)
     copy = pltpu.make_async_copy(clip_ref, index_ref, copied)
     copy.start()
+    segment_ref[...] = jnp.where(wanted >= 0, wanted, ROWS)
+    used = jnp.sum((wanted >= 0).astype(f32), axis=1)
+    count_ref[...] = jnp.broadcast_to(jnp.sum(used, axis=1, keepdims=True), (TABLES, LANES)).astype(i32)
     copy.wait()
     trade(me, 1, TABLES, index_ref, table_ref, block_ref, rows_ref, back_ref, sent, got)
     finish(me, rows_ref, back_ref, sent, got)
@@ -194,15 +200,17 @@
     return pl.pallas_call(
         fetch_kernel,
         out_shape=(
-            jax.ShapeDtypeStruct((FEATS, BATCH), i32),
+            jax.ShapeDtypeStruct((FEATS * BATCH // LANES, LANES), i32),
             jax.ShapeDtypeStruct(lists, i32),
             jax.ShapeDtypeStruct(lists, i32),
+            jax.ShapeDtypeStruct((TABLES, LANES), i32),
             jax.ShapeDtypeStruct((TABLES, CAP, WIDTH), bf16),
         ),
         in_specs=[vmem()] * 3,
-        out_specs=(vmem(),) * 4,
+        out_specs=(vmem(),) * 5,
         scratch_shapes=[
-            pltpu.VMEM((FEATS, BATCH), i32),
+            pltpu.VMEM((FEATS * BATCH // LANES, LANES), i32),
+            pltpu.VMEM(lists, i32),
             pltpu.VMEM(lists, i32),
             pltpu.VMEM(lists, i32),
             pltpu.SMEM(lists, i32),
@@ -273,7 +281,9 @@
     sig_pre = jax.nn.sigmoid(pre_act)
     last = last_ref[...]
     logits = jnp.sum(pre_act * sig_pre * last, axis=1, keepdims=True)
-    residual = jax.nn.sigmoid(logits) - label_ref[...]
+    own = iota((SHARE, LANES), 1) == iota((SHARE, LANES), 0) + lax.rem(me, 2) * SHARE
+    labels = label_ref[pl.ds(me // 2, 1), :].astype(f32)
+    residual = jax.nn.sigmoid(logits) - jnp.sum(jnp.where(own, labels, 0.0), axis=1, keepdims=True)
     slope_ref[mine, :] = (residual * last * (sig_pre * (1.0 + pre_act * (1.0 - sig_pre)))).astype(bf16)
     for d in range(1, GROUPS):
         peer = lax.rem(me + d, GROUPS)
@@ -308,9 +318,23 @@
     )(slot, back, weight, label, last)
 
 
+def pack(total):
+    top = jnp.max(jnp.abs(total), axis=1, keepdims=True)
+    power = jnp.ceil(jnp.log2(jnp.clip(top * 1.0001, 1e-30, 1e30))) - 15.0
+    scaled = jnp.floor(total * jnp.exp2(-power) + 0.5).astype(i32)
+    power = jnp.broadcast_to(power.astype(i32), (OUT_ROWS, LANES))
+    return jnp.concatenate([scaled, power], axis=1).astype(jnp.int16)
+
+
+def unpack(packed):
+    wide = packed.astype(i32).astype(f32)
+    unit = jnp.exp2(wide[:, FEATS * WIDTH :])
+    return wide[:, : FEATS * WIDTH] * jnp.concatenate([unit] * (FEATS * WIDTH // LANES), axis=1)
+
+
 def give_kernel(
     source_ref, slope_ref, pooled_ref, weight_ref, back_ref, packed_ref,
-    table_ref, block_ref, rows_ref, grad_ref, near_ref, across_ref, sent, got, sent_near, got_near, sent_across, got_across,
+    table_ref, block_ref, rows_ref, grad_ref, near_ref, coded_ref, across_ref, sent, got, sent_near, got_near, sent_across, got_across,
 ):
     me = lax.axis_index("table")
     core, side = lax.rem(me, 2), lax.rem(me // 2, 2)
@@ -333,7 +357,7 @@
         return push("table", other, grad_ref.at[z, :, 1 - core], near_ref.at[z], sent_near.at[z], got_near.at[z])
 
     def to_across(z):
-        return push("table", across, grad_ref.at[z, 1 - side, core], across_ref.at[z], sent_across.at[z], got_across.at[z])
+        return push("table", across, coded_ref.at[z], across_ref.at[z], sent_across.at[z], got_across.at[z])
 
     def outer(z, carry):
         at = pl.multiple_of(z * LANES, LANES)
@@ -351,6 +375,7 @@
         to_near(z).wait()
         for x in range(2):
             grad_ref[z, x, core] = grad_ref[z, x, core] + near_ref[z, x]
+        coded_ref[z] = pack(grad_ref[z, 1 - side, core])
         to_across(z).start()
         return carry
 
@@ -358,13 +383,8 @@
 
     def seal(z, carry):
         to_across(z).wait()
-        total = grad_ref[z, side, core] + across_ref[z]
-        top = jnp.max(jnp.abs(total), axis=1, keepdims=True)
-        power = jnp.ceil(jnp.log2(jnp.clip(top * 1.0001, 1e-30, 1e30))) - 15.0
-        scaled = jnp.floor(total * jnp.exp2(-power) + 0.5).astype(i32)
-        k = lax.rem(z - me // NEAR + PLANES, PLANES)
-        packed_ref[k, :, : FEATS * WIDTH] = scaled.astype(jnp.int16)
-        packed_ref[k, :, FEATS * WIDTH :] = jnp.broadcast_to(power.astype(i32), (OUT_ROWS, LANES)).astype(jnp.int16)
+        total = grad_ref[z, side, core] + unpack(across_ref[z])
+        packed_ref[lax.rem(z - me // NEAR + PLANES, PLANES)] = pack(total)
         return carry
 
     lax.fori_loop(0, PLANES, seal, 0)
@@ -373,11 +393,12 @@
 
 def give(source, slope, pooled, weight):
     piece = (OUT_ROWS, FEATS * WIDTH)
+    coded = (PLANES, OUT_ROWS, FEATS * WIDTH + LANES)
     return pl.pallas_call(
         give_kernel,
         out_shape=(
             jax.ShapeDtypeStruct((TABLES, CAP, WIDTH), bf16),
-            jax.ShapeDtypeStruct((PLANES, OUT_ROWS, FEATS * WIDTH + LANES), jnp.int16),
+            jax.ShapeDtypeStruct(coded, jnp.int16),
         ),
         in_specs=[smem(), vmem(), vmem(), vmem()],
         out_specs=(vmem(), vmem()),
@@ -387,7 +408,8 @@
             pltpu.VMEM((TABLES, CAP, WIDTH), bf16),
             pltpu.VMEM((PLANES, 2, 2) + piece, f32),
             pltpu.VMEM((PLANES, 2) + piece, f32),
-            pltpu.VMEM((PLANES,) + piece, f32),
+            pltpu.VMEM(coded, jnp.int16),
+            pltpu.VMEM(coded, jnp.int16),
             dma(TABLES),
             dma(TABLES),
             dma(PLANES),
@@ -400,19 +422,6 @@
     )(source, slope, pooled, weight)
 
 
-def unpack(packed):
-    power = packed[:, FEATS * WIDTH : FEATS * WIDTH + 1].astype(f32)
-    return packed[:, : FEATS * WIDTH].astype(f32) * jnp.exp2(power)
-
-
-def sum_planes(packed):
-    total = unpack(packed[0])
-    for k in range(1, PLANES):
-        ring = [(t, (t + NEAR * k) % TABLES) for t in range(TABLES)]
-        total = total + unpack(lax.ppermute(packed[k], "table", ring))
-    return total
-
-
 def update_kernel(
     index_ref, count_ref, slot_ref, incoming_ref, table_ref, state_ref, rows_ref, new_state_ref, stripes_ref, block_ref, *accs
 ):
@@ -434,7 +443,7 @@
                 accs[j][pl.ds(row, 1), :] = accs[j][pl.ds(row, 1), :] + block_ref[pl.ds(at + j, 1), :]
             return inner
 
-        return lax.fori_loop(0, (count_ref[t] + ACCS - 1) // ACCS, group, carry)
+        return lax.fori_loop(0, (count_ref[t, 0] + ACCS - 1) // ACCS, group, carry)
 
     lax.fori_loop(0, TABLES, peer, 0)
     half = WIDTH // 2
@@ -472,36 +481,63 @@
     )(index, count, slot, incoming, table, state)
 
 
-def stripe_kernel(stripes_ref, parity_ref, out_ref, arrived_ref, sent, got):
+def close_kernel(
+    stripes_ref, parity_ref, packed_ref, out_ref, grad_ref, arrived_ref, landed_ref, sent, got, sent_grad, got_grad
+):
     me = lax.axis_index("group")
+    spot = lax.axis_index("table")
+    plane, q = spot // NEAR, lax.rem(spot, NEAR)
+
+    def along(k):
+        return lax.rem(plane + k, PLANES) * NEAR + q
+
     hail("group", GROUPS)
-    gather_in(GROUPS)
-    copies = []
+    barrier = pltpu.get_barrier_semaphore()
+    for k in range(1, PLANES):
+        pl.semaphore_signal(barrier, inc=1, device_id={"table": along(k)}, device_id_type=MESH)
+    pl.semaphore_wait(barrier, GROUPS + PLANES - 2)
+    shares, copies = [], []
+    for k in sorted(range(1, PLANES), key=lambda k: min(k, PLANES - k)):
+        shares.append(push("table", along(k), packed_ref.at[k], landed_ref.at[k], sent_grad.at[k], got_grad.at[k]))
+        shares[-1].start()
     for d in range(1, GROUPS):
         peer = lax.rem(me + d, GROUPS)
         theirs = stripes_ref.at[pl.ds(peer * OWNED, OWNED)]
         copies.append(push("group", peer, theirs, arrived_ref.at[d], sent.at[d], got.at[d]))
         copies[-1].start()
     total = stripes_ref[pl.ds(me * OWNED, OWNED)].astype(f32)
+    grad_ref[...] = unpack(packed_ref[0])
     for copy in copies:
-        copy.wait_recv()
+        copy.wait()
     for d in range(1, GROUPS):
         total = total + arrived_ref[d].astype(f32)
     out_ref[...] = parity_ref[...] + total
-    for copy in copies:
-        copy.wait_send()
-
-
-def stripe_sum(stripes, parity):
+    for copy in shares:
+        copy.wait()
+    for k in range(1, PLANES):
+        grad_ref[...] = grad_ref[...] + unpack(landed_ref[k])
+
+
+def close(stripes, parity, packed):
     return pl.pallas_call(
-        stripe_kernel,
-        out_shape=jax.ShapeDtypeStruct(parity.shape, f32),
-        in_specs=[vmem()] * 2,
-        out_specs=vmem(),
-        scratch_shapes=[pltpu.VMEM((GROUPS,) + parity.shape, bf16)] + [pltpu.SemaphoreType.DMA((GROUPS,))] * 2,
+        close_kernel,
+        out_shape=(
+            jax.ShapeDtypeStruct(parity.shape, f32),
+            jax.ShapeDtypeStruct((OUT_ROWS, FEATS * WIDTH), f32),
+        ),
+        in_specs=[vmem()] * 3,
+        out_specs=(vmem(), vmem()),
+        scratch_shapes=[
+            pltpu.VMEM((GROUPS,) + parity.shape, bf16),
+            pltpu.VMEM(packed.shape, jnp.int16),
+            dma(GROUPS),
+            dma(GROUPS),
+            dma(PLANES),
+            dma(PLANES),
+        ],
         compiler_params=params(1),
-        name="stripe_sum",
-    )(stripes, parity)
+        name="close",
+    )(stripes, parity, packed)
 
 
 def local(
@@ -516,19 +552,15 @@
     last_weight,
 ):
     table = table_rows[0]
-    target = jnp.transpose(row_shard[0, :, :, 0])
+    target = jnp.transpose(row_shard.reshape(BATCH // LANES, LANES, FEATS), (2, 0, 1)).reshape(-1, LANES)
     offset = jnp.transpose(row_offset[0])
-    slot, source, wanted, back = fetch(target, offset, table)
-    own = lax.dynamic_slice(labels, (lax.axis_index("group") * SHARE,), (SHARE,)).astype(f32)
-    pooled, slope = mix(slot.reshape(-1), back, first_weight, own[:, None], last_weight[None, :])
+    slot, source, segment, served, back = fetch(target, offset, table)
+    pooled, slope = mix(slot.reshape(-1), back, first_weight, labels.reshape(-1, LANES), last_weight[None, :])
     incoming, packed = give(source, slope, pooled, first_weight)
-    first_grad = sum_planes(packed)
-    served = jnp.sum((wanted >= 0).astype(i32), axis=(1, 2))
-    segment = jnp.where(wanted >= 0, wanted, ROWS).reshape(-1)
     new_rows, new_state, stripes = update(
-        segment, served, parity_slot[0], incoming, table, row_state.reshape(ROWS // WIDTH, WIDTH)
+        segment.reshape(-1), served, parity_slot[0], incoming, table, row_state.reshape(ROWS // WIDTH, WIDTH)
     )
-    new_parity = stripe_sum(stripes, parity[0])
+    new_parity, first_grad = close(stripes, parity[0], packed)
     return (new_rows[None], new_state.reshape(1, ROWS), new_parity[None], first_grad)
 
 

time: 385 us -> 361 us (0.938)
  starting transfers between devices: 20.1 us -> 0 us
  Pallas kernels: 345 us -> 351 us
  waiting for transfers between devices: 5.63 us -> 0 us
  other arithmetic: 4.56 us -> 0 us
    pallas_call x2, Pallas kernels: 132 us -> 161 us  [the longest x1 119 us: fetch(): pl.pallas_call(fetch_kernel, out_shape=(jax.ShapeDtypeStruct((FEATS * BAT...]
    pallas_call x1, Pallas kernels: 140 us -> 119 us  [give(): pl.pallas_call(give_kernel, out_shape=(jax.ShapeDtypeStruct((TABLES, CAP,...]
    ppermute x7 -> x0, starting transfers between devices: 20.1 us -> none  [sum_planes(): total = total + unpack(lax.ppermute(packed[k], 'table', ring))]
    ppermute x7 -> x0, waiting for transfers between devices: 5.63 us -> none  [sum_planes(): total = total + unpack(lax.ppermute(packed[k], 'table', ring))]
  transfers between devices with their start and end apart: 7 -> 0, of which waited for: 2 -> 0; matrix products, arithmetic and copies ran while one was open for 1% -> 0% of each run, Pallas kernels for 8% -> 0%
where the time goes in v5:
time: 361 us; the launch traced here: 355 us
  Pallas kernels  351 us (97%)
    pallas_call x1, Pallas kernels, fetch(): pl.pallas_call(fetch_kernel, out_shape=(jax.ShapeDtypeStruct((FEATS * BAT...  119 us
    pallas_call x1, Pallas kernels, give(): pl.pallas_call(give_kernel, out_shape=(jax.ShapeDtypeStruct((TABLES, CAP,...  119 us
    pallas_call x1, Pallas kernels, mix(): pl.pallas_call(mix_kernel, out_shape=(jax.ShapeDtypeStruct((BATCH, FEATS...  54 us
    pallas_call x1, Pallas kernels, close(): pl.pallas_call(close_kernel, out_shape=(jax.ShapeDtypeStruct(parity.shape...  41.2 us
    pallas_call x1, Pallas kernels, update(): pl.pallas_call(update_kernel, out_shape=(jax.ShapeDtypeStruct((ROWS, WIDT...  17.8 us

profile of v5, /device:TPU:16, one launch (start us, length us, event | category | flops | bytes accessed | tf_op | source)
XLA Modules:
  0.0 354.9 jit_solution(5964927919935484518)
XLA Ops:
  0.6 119.4 %fetch.1 = (s32[64,128]{1,0:T(8,128)}, s32[32,4,128]{2,1,0:T(4,128)}, s32[32,4,128]{2,1,0:T(4,128)}, s32[32,128]{1,0:T(8,128)}, bf16[32,512,128]{2,1,0:T(8,128)(2,1)}) custom-call(s32[64,128]{1,0:T(8,128)} %bitcast.24, s32[16,512]{1,0:T(8,128)} %bitcast.25, f32[4096,128]{1,0:T(8,128)} %bitcast.19), custom_call_target="tpu_custom_call" | custom-call | tf_op jit(solution)/shard_map/fetch/pallas_call | solution.py:200
  120.1 54.0 %mix.1 = (bf16[512,2048]{1,0:T(8,128)(2,1)}, bf16[512,1024]{1,0:T(8,128)(2,1)}) custom-call(s32[8192]{0:T(1024)} %bitcast.26, bf16[32,512,128]{2,1,0:T(8,128)(2,1)} %get-tuple-element.22.back_ref, bf16[2048,1024]{1,0:T(8,128)(2,1)} %weight_ref.3, s32[4,128]{1,0:T(4,128)} %bitcast.29, f32[1,1024]{1,0:T(1,128)} %bitcast.28), custom_call_target="tpu_custom_call" | custom-call | tf_op jit(solution)/shard_map/mix/pallas_call | solution.py:298
  174.0 118.6 %give.1 = (bf16[32,512,128]{2,1,0:T(8,128)(2,1)}, s16[8,32,2176]{2,1,0:T(8,128)(2,1)}) custom-call(s32[32,4,128]{2,1,0:T(4,128)} %get-tuple-element.20.source_ref, bf16[512,1024]{1,0:T(8,128)(2,1)} %get-tuple-element.23.slope_ref, bf16[512,2048]{1,0:T(8,128)(2,1)} %get-tuple-element.24.pooled_ref, bf16[2048,1024]{1,0:T(8,128)(2,1)} %weight_ref.3), custom_call_target="tpu_custom_call" | custom-call | tf_op jit(solution)/shard_map/give/pallas_call | solution.py:397
  292.6 17.8 %update.1 = (f32[4096,128]{1,0:T(8,128)}, f32[32,128]{1,0:T(8,128)}, bf16[32,64,128]{2,1,0:T(8,128)(2,1)}) custom-call(s32[16384]{0:T(1024)} %bitcast.23, s32[32,128]{1,0:T(8,128)} %get-tuple-element.19.count_ref, s32[32]{0:T(128)} %bitcast.30, bf16[32,512,128]{2,1,0:T(8,128)(2,1)} %get-tuple-element.25.incoming_ref, f32[4096,128]{1,0:T(8,128)} %bitcast.20, ...), custom_call_target="tpu_custom_call" | custom-call | tf_op jit(solution)/shard_map/update/pallas_call | solution.py:469
  310.4 41.2 %close.1 = (f32[4,64,128]{2,1,0:T(8,128)}, f32[32,2048]{1,0:T(8,128)}) custom-call(bf16[32,64,128]{2,1,0:T(8,128)(2,1)} %get-tuple-element.28.stripes_ref, f32[4,64,128]{2,1,0:T(8,128)} %bitcast.21, s16[8,32,2176]{2,1,0:T(8,128)(2,1)} %get-tuple-element.29.packed_ref), custom_call_target="tpu_custom_call" | custom-call | tf_op jit(solution)/shard_map/close/pallas_call | solution.py:522
  351.6 1.6 copy.15
  353.2 1.7 copy.16

commit v6 on v5

--- a/solution.py
+++ b/solution.py
@@ -20,7 +20,8 @@
 NEAR = 4
 PLANES = TABLES // NEAR
 OUT_ROWS = HIDDEN // TABLES
-EARLY = 9
+EARLY = 5
+MIDWAY = 17
 SHARE = BATCH // GROUPS
 OWNED = 32 // GROUPS
 LANES = 128
@@ -106,11 +107,11 @@
         first = jnp.where(named, f + 1 + 32 * (sample // 256), 0)
         second = jnp.where(named, jnp.broadcast_to(offset_ref[pl.ds(f, 1), :], named.shape), 0)
         third = jnp.where(named, sample % 256, 0)
-        values = jnp.concatenate([first, second, third], axis=0).astype(f32).astype(bf16)
+        values = jnp.concatenate([first, second, third, third], axis=0).astype(f32).astype(bf16)
         chosen = (line(rank_ref, f) == spot).astype(f32).astype(bf16)
-        return total + dot_nt(values, chosen)
-
-    total = lax.fori_loop(0, FEATS, feature, jnp.zeros((3 * TABLES, CAP), f32)).astype(i32)
+        return total + dot_nt(chosen, values)
+
+    total = lax.fori_loop(0, FEATS, feature, jnp.zeros((CAP, 4 * TABLES), f32)).T.astype(i32)
     first, second, third = (total[k * TABLES : (k + 1) * TABLES] for k in range(3))
     used = first > 0
     f = first % 32 - 1
@@ -333,11 +334,12 @@
 
 
 def give_kernel(
-    source_ref, slope_ref, pooled_ref, weight_ref, back_ref, packed_ref,
-    table_ref, block_ref, rows_ref, grad_ref, near_ref, coded_ref, across_ref, sent, got, sent_near, got_near, sent_across, got_across,
+    source_ref, slope_ref, pooled_ref, weight_ref, back_ref, total_ref,
+    table_ref, block_ref, rows_ref, grad_ref, near_ref, coded_ref, across_ref, packed_ref, landed_ref,
+    sent, got, sent_near, got_near, sent_across, got_across, sent_along, got_along,
 ):
     me = lax.axis_index("table")
-    core, side = lax.rem(me, 2), lax.rem(me // 2, 2)
+    core, side, plane, q = lax.rem(me, 2), lax.rem(me // 2, 2), me // NEAR, lax.rem(me, NEAR)
     other, across = me + 1 - 2 * core, me + 2 - 4 * side
     hail("table", TABLES)
 
@@ -359,7 +361,16 @@
     def to_across(z):
         return push("table", across, coded_ref.at[z], across_ref.at[z], sent_across.at[z], got_across.at[z])
 
-    def outer(z, carry):
+    def to_along(k):
+        peer = lax.rem(plane + k, PLANES) * NEAR + q
+        return push("table", peer, packed_ref.at[k], landed_ref.at[k], sent_along.at[k], got_along.at[k])
+
+    def ahead(turn):
+        by = (PLANES - turn) // 2 * (1 - 2 * lax.rem(turn, 2))
+        return lax.rem(by + PLANES, PLANES)
+
+    def outer(turn, carry):
+        z = lax.rem(plane + ahead(turn), PLANES)
         at = pl.multiple_of(z * LANES, LANES)
         part = lax.dot_general(
             slope_ref[:, pl.ds(at, LANES)], pooled_ref[...], (((0,), (0,)), ((), ())), preferred_element_type=f32
@@ -369,9 +380,10 @@
         return carry
 
     lax.fori_loop(0, PLANES, outer, 0)
-    trade(me, EARLY, TABLES, source_ref, table_ref, block_ref, rows_ref, back_ref, sent, got)
-
-    def fold(z, carry):
+    trade(me, EARLY, MIDWAY, source_ref, table_ref, block_ref, rows_ref, back_ref, sent, got)
+
+    def fold(turn, carry):
+        z = lax.rem(plane + ahead(turn), PLANES)
         to_near(z).wait()
         for x in range(2):
             grad_ref[z, x, core] = grad_ref[z, x, core] + near_ref[z, x]
@@ -380,15 +392,28 @@
         return carry
 
     lax.fori_loop(0, PLANES, fold, 0)
-
-    def seal(z, carry):
+    trade(me, MIDWAY, TABLES, source_ref, table_ref, block_ref, rows_ref, back_ref, sent, got)
+
+    def seal(turn, carry):
+        k = ahead(turn)
+        z = lax.rem(plane + k, PLANES)
         to_across(z).wait()
-        total = grad_ref[z, side, core] + unpack(across_ref[z])
-        packed_ref[lax.rem(z - me // NEAR + PLANES, PLANES)] = pack(total)
-        return carry
-
-    lax.fori_loop(0, PLANES, seal, 0)
+        packed_ref[k] = pack(grad_ref[z, side, core] + unpack(across_ref[z]))
+        to_along(k).start()
+        return carry
+
+    lax.fori_loop(0, PLANES - 1, seal, 0)
+    to_across(plane).wait()
+    total_ref[...] = grad_ref[plane, side, core] + unpack(across_ref[plane])
     finish(me, rows_ref, back_ref, sent, got)
+
+    def land(turn, carry):
+        k = ahead(turn)
+        to_along(k).wait()
+        total_ref[...] = total_ref[...] + unpack(landed_ref[k])
+        return carry
+
+    lax.fori_loop(0, PLANES - 1, land, 0)
 
 
 def give(source, slope, pooled, weight):
@@ -398,7 +423,7 @@
         give_kernel,
         out_shape=(
             jax.ShapeDtypeStruct((TABLES, CAP, WIDTH), bf16),
-            jax.ShapeDtypeStruct(coded, jnp.int16),
+            jax.ShapeDtypeStruct(piece, f32),
         ),
         in_specs=[smem(), vmem(), vmem(), vmem()],
         out_specs=(vmem(), vmem()),
@@ -410,8 +435,12 @@
             pltpu.VMEM((PLANES, 2) + piece, f32),
             pltpu.VMEM(coded, jnp.int16),
             pltpu.VMEM(coded, jnp.int16),
+            pltpu.VMEM(coded, jnp.int16),
+            pltpu.VMEM(coded, jnp.int16),
             dma(TABLES),
             dma(TABLES),
+            dma(PLANES),
+            dma(PLANES),
             dma(PLANES),
             dma(PLANES),
             dma(PLANES),
@@ -481,63 +510,36 @@
     )(index, count, slot, incoming, table, state)
 
 
-def close_kernel(
-    stripes_ref, parity_ref, packed_ref, out_ref, grad_ref, arrived_ref, landed_ref, sent, got, sent_grad, got_grad
-):
+def stripe_kernel(stripes_ref, parity_ref, out_ref, arrived_ref, sent, got):
     me = lax.axis_index("group")
-    spot = lax.axis_index("table")
-    plane, q = spot // NEAR, lax.rem(spot, NEAR)
-
-    def along(k):
-        return lax.rem(plane + k, PLANES) * NEAR + q
-
     hail("group", GROUPS)
-    barrier = pltpu.get_barrier_semaphore()
-    for k in range(1, PLANES):
-        pl.semaphore_signal(barrier, inc=1, device_id={"table": along(k)}, device_id_type=MESH)
-    pl.semaphore_wait(barrier, GROUPS + PLANES - 2)
-    shares, copies = [], []
-    for k in sorted(range(1, PLANES), key=lambda k: min(k, PLANES - k)):
-        shares.append(push("table", along(k), packed_ref.at[k], landed_ref.at[k], sent_grad.at[k], got_grad.at[k]))
-        shares[-1].start()
+    gather_in(GROUPS)
+    copies = []
     for d in range(1, GROUPS):
         peer = lax.rem(me + d, GROUPS)
         theirs = stripes_ref.at[pl.ds(peer * OWNED, OWNED)]
         copies.append(push("group", peer, theirs, arrived_ref.at[d], sent.at[d], got.at[d]))
         copies[-1].start()
     total = stripes_ref[pl.ds(me * OWNED, OWNED)].astype(f32)
-    grad_ref[...] = unpack(packed_ref[0])
     for copy in copies:
-        copy.wait()
+        copy.wait_recv()
     for d in range(1, GROUPS):
         total = total + arrived_ref[d].astype(f32)
     out_ref[...] = parity_ref[...] + total
-    for copy in shares:
-        copy.wait()
-    for k in range(1, PLANES):
-        grad_ref[...] = grad_ref[...] + unpack(landed_ref[k])
-
-
-def close(stripes, parity, packed):
+    for copy in copies:
+        copy.wait_send()
+
+
+def stripe_sum(stripes, parity):
     return pl.pallas_call(
-        close_kernel,
-        out_shape=(
-            jax.ShapeDtypeStruct(parity.shape, f32),
-            jax.ShapeDtypeStruct((OUT_ROWS, FEATS * WIDTH), f32),
-        ),
-        in_specs=[vmem()] * 3,
-        out_specs=(vmem(), vmem()),
-        scratch_shapes=[
-            pltpu.VMEM((GROUPS,) + parity.shape, bf16),
-            pltpu.VMEM(packed.shape, jnp.int16),
-            dma(GROUPS),
-            dma(GROUPS),
-            dma(PLANES),
-            dma(PLANES),
-        ],
+        stripe_kernel,
+        out_shape=jax.ShapeDtypeStruct(parity.shape, f32),
+        in_specs=[vmem()] * 2,
+        out_specs=vmem(),
+        scratch_shapes=[pltpu.VMEM((GROUPS,) + parity.shape, bf16)] + [pltpu.SemaphoreType.DMA((GROUPS,))] * 2,
         compiler_params=params(1),
-        name="close",
-    )(stripes, parity, packed)
+        name="stripe_sum",
+    )(stripes, parity)
 
 
 def local(
@@ -556,11 +558,11 @@
     offset = jnp.transpose(row_offset[0])
     slot, source, segment, served, back = fetch(target, offset, table)
     pooled, slope = mix(slot.reshape(-1), back, first_weight, labels.reshape(-1, LANES), last_weight[None, :])
-    incoming, packed = give(source, slope, pooled, first_weight)
+    incoming, first_grad = give(source, slope, pooled, first_weight)
     new_rows, new_state, stripes = update(
         segment.reshape(-1), served, parity_slot[0], incoming, table, row_state.reshape(ROWS // WIDTH, WIDTH)
     )
-    new_parity, first_grad = close(stripes, parity[0], packed)
+    new_parity = stripe_sum(stripes, parity[0])
     return (new_rows[None], new_state.reshape(1, ROWS), new_parity[None], first_grad)
 
 

time: 361 us -> 365 us (1.011); the launches traced: 355 us -> 364 us
  Pallas kernels: 351 us -> 361 us
    pallas_call x1, Pallas kernels: 41.2 us -> 16.4 us  [stripe_sum(): pl.pallas_call(stripe_kernel, out_shape=jax.ShapeDtypeStruct(parity.shape...]
    pallas_call x1, Pallas kernels: 119 us -> 139 us  [give(): pl.pallas_call(give_kernel, out_shape=(jax.ShapeDtypeStruct((TABLES, CAP,...]
    pallas_call x1, Pallas kernels: 17.8 us -> 32.1 us  [update(): pl.pallas_call(update_kernel, out_shape=(jax.ShapeDtypeStruct((ROWS, WIDT...]
where the time goes in v6:
time: 365 us; the launch traced here: 364 us
  Pallas kernels  361 us (99%)
    pallas_call x1, Pallas kernels, give(): pl.pallas_call(give_kernel, out_shape=(jax.ShapeDtypeStruct((TABLES, CAP,...  139 us
    pallas_call x1, Pallas kernels, fetch(): pl.pallas_call(fetch_kernel, out_shape=(jax.ShapeDtypeStruct((FEATS * BAT...  120 us
    pallas_call x1, Pallas kernels, mix(): pl.pallas_call(mix_kernel, out_shape=(jax.ShapeDtypeStruct((BATCH, FEATS...  53.9 us
    pallas_call x1, Pallas kernels, update(): pl.pallas_call(update_kernel, out_shape=(jax.ShapeDtypeStruct((ROWS, WIDT...  32.1 us
    pallas_call x1, Pallas kernels, stripe_sum(): pl.pallas_call(stripe_kernel, out_shape=jax.ShapeDtypeStruct(parity.shape...  16.4 us

profile of v6, /device:TPU:16, one launch (start us, length us, event | category | flops | bytes accessed | tf_op | source)
XLA Modules:
  0.0 363.9 jit_solution(9680889102957702575)
XLA Ops:
  0.6 119.9 %fetch.1 = (s32[64,128]{1,0:T(8,128)}, s32[32,4,128]{2,1,0:T(4,128)}, s32[32,4,128]{2,1,0:T(4,128)}, s32[32,128]{1,0:T(8,128)}, bf16[32,512,128]{2,1,0:T(8,128)(2,1)}) custom-call(s32[64,128]{1,0:T(8,128)} %bitcast.24, s32[16,512]{1,0:T(8,128)} %bitcast.25, f32[4096,128]{1,0:T(8,128)} %bitcast.19), custom_call_target="tpu_custom_call" | custom-call | tf_op jit(solution)/shard_map/fetch/pallas_call | solution.py:201
  120.5 53.9 %mix.1 = (bf16[512,2048]{1,0:T(8,128)(2,1)}, bf16[512,1024]{1,0:T(8,128)(2,1)}) custom-call(s32[8192]{0:T(1024)} %bitcast.26, bf16[32,512,128]{2,1,0:T(8,128)(2,1)} %get-tuple-element.20.back_ref, bf16[2048,1024]{1,0:T(8,128)(2,1)} %weight_ref.3, s32[4,128]{1,0:T(4,128)} %bitcast.29, f32[1,1024]{1,0:T(1,128)} %bitcast.28), custom_call_target="tpu_custom_call" | custom-call | tf_op jit(solution)/shard_map/mix/pallas_call | solution.py:299
  174.4 138.7 %give.1 = (bf16[32,512,128]{2,1,0:T(8,128)(2,1)}, f32[32,2048]{1,0:T(8,128)}) custom-call(s32[32,4,128]{2,1,0:T(4,128)} %get-tuple-element.18.source_ref, bf16[512,1024]{1,0:T(8,128)(2,1)} %get-tuple-element.21.slope_ref, bf16[512,2048]{1,0:T(8,128)(2,1)} %get-tuple-element.22.pooled_ref, bf16[2048,1024]{1,0:T(8,128)(2,1)} %weight_ref.3), custom_call_target="tpu_custom_call" | custom-call | tf_op jit(solution)/shard_map/give/pallas_call | solution.py:422
  313.1 0.0 copy-start
  313.1 32.1 %update.1 = (f32[4096,128]{1,0:T(8,128)}, f32[32,128]{1,0:T(8,128)}, bf16[32,64,128]{2,1,0:T(8,128)(2,1)}) custom-call(s32[16384]{0:T(1024)} %bitcast.23, s32[32,128]{1,0:T(8,128)} %get-tuple-element.17.count_ref, s32[32]{0:T(128)} %bitcast.30, bf16[32,512,128]{2,1,0:T(8,128)(2,1)} %get-tuple-element.23.incoming_ref, f32[4096,128]{1,0:T(8,128)} %bitcast.20, ...), custom_call_target="tpu_custom_call" | custom-call | tf_op jit(solution)/shard_map/update/pallas_call | solution.py:498
  345.3 16.4 %stripe_sum.1 = f32[4,64,128]{2,1,0:T(8,128)} custom-call(bf16[32,64,128]{2,1,0:T(8,128)(2,1)} %get-tuple-element.26.stripes_ref, f32[4,64,128]{2,1,0:T(8,128)} %bitcast.22), custom_call_target="tpu_custom_call" | custom-call | tf_op jit(solution)/shard_map/stripe_sum/pallas_call | solution.py:534
  361.7 1.6 copy.15
  363.2 0.0 copy-done
  363.2 0.7 copy.16
Async XLA Ops:
  313.1 50.1 %copy-start = (f32[32,2048]{1,0:T(8,128)S(1)}, f32[32,2048]{1,0:T(8,128)}, u32[]{:S(2)}) copy-start(f32[32,2048]{1,0:T(8,128)} %get-tuple-element.35) | copy-start | bytes 786436
